TPU v7x, 32 devices: a whole 2x2x4 slice. The times are simulated.
32 devices in a mesh: grp: 4 (over x, core), vocab: 8 (over z, y).
Axes of the slice: x: 2, y: 2, z: 4, core: 2. Of those that a mesh axis runs over, the one named last changes fastest.
Arguments:
- hidden: bfloat16 [256, 4096], P(('grp', 'vocab')), parts along dimension 0
- head: bfloat16 [4096, 24576], P(None, 'vocab'), may hold values from -0.09375 to 0.09375
- block_ids: int32 [256, 16], P('grp'), parts along dimension 0, may hold values from 0 to 191, as said below
- valid_count: int32 [256], P('grp'), parts along dimension 0, may hold values from 1 to 16, as said below
- beam_order: int32 [256], P('grp'), parts along dimension 0, may hold values from 0 to 63, each once
Outputs:
- block_logprobs: float32 [256, 16, 128], P(('grp', 'vocab')), parts along dimension 0
There are 4 independent parts, one for each index of `grp`. A program takes and returns all parts, laid end to end along the dimension named above; an argument that names none is the same for every part. Nothing has to cross between parts.
Inputs may be any that keep to these rules, and one draw needn't show every extreme that they name: `block_ids`: vocabulary block b holds entries 128 * b to 128 * b + 127 and lies on vocabulary device b // 24. Among the 128 slots of the output rows of one vocabulary device, at most 16 name blocks of any one vocabulary device, and exactly 16 do for one of them. `valid_count`: some output row has all 16 slots valid.
All inputs are finite; a program needn't handle non-finite values.
Results may differ from a plain program's by a relative error of at most 0.0003.
Values may be sent and summed in bfloat16 or wider, within the bound.
No kernel may reach another device: no remote copies, remote signals or barrier semaphores. Data moves between devices by JAX's collectives and lax.ppermute only.
A program may use at most 128 MiB of HBM per device.

v0:
```python
import jax
import jax.numpy as jnp
from jax import lax
from jax.sharding import PartitionSpec as P

BLK = 128


def body(hidden, head, block_ids, valid_count, beam_order):
    me_dev = lax.axis_index("vocab")
    beams = block_ids.shape[0]
    kslots = block_ids.shape[1]
    blocks_dev = head.shape[1] // BLK
    logits = jnp.dot(
        lax.all_gather(hidden, "vocab", axis=0, tiled=True),
        head,
        preferred_element_type=jnp.float32,
    )
    local_max = jnp.max(logits, axis=1)
    top = lax.pmax(local_max, "vocab")
    total = lax.psum(jnp.sum(jnp.exp(logits - top[:, None]), axis=1), "vocab")
    lse = top + jnp.log(total)
    ordered = logits[beam_order].reshape(beams, blocks_dev, BLK)
    owner_dev = block_ids // blocks_dev
    local_block = block_ids % blocks_dev
    row_index = jnp.arange(beams, dtype=jnp.int32)[:, None]
    tiles = ordered[row_index, local_block] - lse[beam_order][:, None, None]
    slot_index = jnp.arange(kslots, dtype=jnp.int32)[None, :]
    valid = slot_index < valid_count[:, None]
    mine = (owner_dev == me_dev) & valid
    term = jnp.where(mine[:, :, None], tiles, jnp.float32(0.0))
    return lax.psum_scatter(term, "vocab", scatter_dimension=0, tiled=True)


def solution(mesh):
    return jax.shard_map(
        body,
        mesh=mesh,
        in_specs=(P(("grp", "vocab"), None), P(None, "vocab"), P("grp", None), P("grp"), P("grp")),
        out_specs=P(("grp", "vocab"), None, None),
        check_vma=False,
    )
```

profile of v0, /device:TPU:0, one launch (start us, length us, event | category | flops | bytes accessed | tf_op | source)
XLA Modules:
  0.0 167.4 jit_solution(18439318972249857098)
XLA Ops:
  6.5 0.0 copy-start.2
  6.5 0.0 copy-start
  6.5 0.0 copy-start.1
  6.5 0.0 reduce-scatter.2.cloned.1.call-start
  6.5 33.3 %all_gather.3 = bf16[64,4096]{1,0:T(8,128)(2,1)S(1)} all-gather(bf16[8,4096]{1,0:T(8,128)(2,1)} %param.5), channel_id=1, replica_groups=mesh['grp'=4,'vocab'=8] {'vocab'}, dimensions={0}, use_global_device_ids=true | all-gather | bytes 589824 | tf_op jit(solution)/shard_map/all_gather | solution.py:15
  39.9 10.5 %fusion.7 = (f32[64]{0:T(128)S(1)}, f32[64,3072]{1,0:T(8,128)S(1)}) fusion(bf16[64,4096]{1,0:T(8,128)(2,1)S(1)} %all_gather.3, bf16[4096,3072]{1,0:T(8,128)(2,1)} %param.6), kind=kOutput, calls=%fused_computation.21 | convolution fusion | flops 1610809344 | bytes 26476800 | tf_op jit(solution)/shard_map/dot_general | solution.py:14
  50.4 21.5 %pmax.7 = f32[64]{0:T(128)S(1)} all-reduce(f32[64]{0:T(128)S(1)} %get-tuple-element.5), channel_id=1, replica_groups=mesh['grp'=4,'vocab'=8] {'vocab'}, use_global_device_ids=true, to_apply=%region_1.0 | all-reduce | flops 64 | bytes 512 | tf_op jit(solution)/shard_map/pmax | solution.py:20
  72.0 0.3 exponential_reduce_fusion
  72.3 17.1 %psum.7 = f32[64]{0:T(128)S(1)} all-reduce(f32[64]{0:T(128)S(1)} %exponential_reduce_fusion), channel_id=1, replica_groups=mesh['grp'=4,'vocab'=8] {'vocab'}, use_global_device_ids=true, to_apply=%region_3.0 | all-reduce | flops 64 | bytes 512 | tf_op jit(solution)/shard_map/psum | solution.py:21
  89.4 0.0 copy-done.2
  89.4 0.8 gather_fusion
  90.3 0.8 gather_fusion.2
  91.0 0.1 copy.9
  91.2 0.0 copy-done
  91.2 0.1 copy.8
  91.3 0.1 reshape.18
  91.4 0.0 copy-done.1
  91.4 0.1 copy.7
  91.5 6.8 %gather_fusion.1 = f32[1024,128]{1,0:T(8,128)S(1)} fusion(f32[64,24,128]{2,1,0:T(8,128)S(1)} %bitcast.11, s32[1024]{0:T(1024)S(1)} %reshape.18), kind=kCustom, calls=%fused_computation.1 | custom fusion | bytes 1056768 | tf_op jit(solution)/shard_map/gather | solution.py:27
  98.3 1.1 subtract_select_fusion
  99.4 0.0 reduce-scatter.2.cloned.1.call-update
  99.4 61.2 %reduce-scatter.2.cloned.1.call-done = f32[8,16,128]{2,1,0:T(8,128)} async-done(((f32[64,16,128]{2,1,0:T(8,128)}), f32[8,16,128]{2,1,0:T(8,128)}) %reduce-scatter.2.cloned.1.call-update) | async-done | bytes 65552 | tf_op jit(solution)/shard_map/reduce_scatter | solution.py:32
  (5 shorter events, 0.1 us)
Async XLA Ops:
  6.5 82.9 %copy-start.2 = (s32[64]{0:T(128)S(1)}, s32[64]{0:T(128)}, u32[]{:S(2)}) copy-start(s32[64]{0:T(128)} %param.9) | copy-start | bytes 772
  6.5 84.6 %copy-start = (s32[64,16]{0,1:T(8,128)S(1)}, s32[64,16]{0,1:T(8,128)}, u32[]{:S(2)}) copy-start(s32[64,16]{0,1:T(8,128)} %param.7) | copy-start | bytes 12292
  6.5 84.8 %copy-start.1 = (s32[64]{0:T(128)S(1)}, s32[64]{0:T(128)}, u32[]{:S(2)}) copy-start(s32[64]{0:T(128)} %param.8) | copy-start | bytes 772
  6.5 154.1 %reduce-scatter.2.cloned.1.call-start = ((), (), s32[]{:S(2)}) async-start(), calls=%async_computation.1 | async-start | bytes 589824 | tf_op jit(solution)/shard_map/reduce_scatter | solution.py:32
Sparse Core Ops, SparseCore 0:
  99.5 61.0 reduce-scatter.1
where the time goes:
time: 168 us; the launch traced here: 167 us
  blocking collectives  72 us (43%)
  waiting for transfers between devices  61.2 us (36%)
  between operations  13.4 us (8%)
  matrix products  10.5 us (6%)
  local copies, waits for them, and re-layouts  8.83 us (5%)
    reduce_scatter x1, waiting for transfers between devices, body(): return lax.psum_scatter(term, 'vocab', scatter_dimension=0, tiled=True)  61.2 us
    all_gather x1, blocking collectives, body(): lax.all_gather(hidden, 'vocab', axis=0, tiled=True)  33.3 us
    pmax x1, blocking collectives, body(): top = lax.pmax(local_max, 'vocab')  21.5 us
    psum x1, blocking collectives, body(): total = lax.psum(jnp.sum(jnp.exp(logits - top[:, None]), axis=1), 'vocab')  17.1 us
    dot_general x1, matrix products, body(): jnp.dot(lax.all_gather(hidden, 'vocab', axis=0, tiled=True), head, prefer...  10.5 us
    gather x2, local copies, waits for them, and re-layouts, body(): tiles = ordered[row_index, local_block] - lse[beam_order][:, None, None]  7.57 us
  transfers between devices with their start and end apart: 1, of which 1 were waited for; matrix products, arithmetic and copies ran while one was open for 0% of the time, Pallas kernels for 0%

commit v1 on v0

v1 whole, which is shorter than its diff:
```python
import functools

import jax
import jax.numpy as jnp
from jax import lax
from jax.experimental import pallas as pl
from jax.experimental.pallas import tpu as pltpu
from jax.sharding import PartitionSpec as P

BLK = 128
CAP = 16
NEAR = 4


def exchange(x, n, mask):
    return lax.ppermute(x, "vocab", [(i, i ^ mask) for i in range(n)])


def score_kernel(n, rows_dev, me_ref, src_ref, order_ref, near_ref, far_ref, head_ref, *refs):
    outs, (x, logits, stats) = refs[:NEAR], refs[NEAR:]
    half = near_ref.shape[0]
    beams = 2 * half
    blocks = head_ref.shape[1] // BLK
    group = 8 if blocks % 8 == 0 else 1
    x[:half, :] = near_ref[...]
    x[half:, :] = far_ref[...]
    for j in range(0, blocks, group):
        product = jnp.dot(x[...], head_ref[:, j * BLK : (j + group) * BLK], preferred_element_type=jnp.float32)
        for i in range(group):
            logits[(j + i) * beams : (j + i + 1) * beams, :] = product[:, i * BLK : (i + 1) * BLK]
    most = functools.reduce(jnp.maximum, [logits[j * beams : (j + 1) * beams, :] for j in range(blocks)])
    most = jnp.max(most, axis=1, keepdims=True)
    total = sum(jnp.exp(logits[j * beams : (j + 1) * beams, :] - most) for j in range(blocks))
    lse = most + jnp.log(jnp.sum(total, axis=1, keepdims=True))
    stats[...] = jnp.broadcast_to(lse, (beams, BLK))
    me = me_ref[0]
    for near in range(NEAR):
        for far in range(n // NEAR):
            owner = me ^ (far * NEAR + near)
            for k in range(CAP):
                outs[near][far, k : k + 1, :] = logits[pl.ds(src_ref[owner * CAP + k], 1), :]
            for i in range(rows_dev):
                outs[near][far, CAP + i : CAP + i + 1, :] = stats[pl.ds(order_ref[owner * rows_dev + i], 1), :]


def place_kernel(n, rows_dev, slots, at_ref, *refs):
    own, others, out_ref, held = refs[:NEAR], refs[NEAR : NEAR + n // NEAR - 1], refs[-2], refs[-1]
    size = CAP + rows_dev
    for near in range(NEAR):
        held[near * size : (near + 1) * size, :] = own[near][0]
        for far in range(1, n // NEAR):
            base = (far * NEAR + near) * size
            held[base : base + size, :] = others[far - 1][near]
    parts = [held[d * size + CAP : (d + 1) * size, :] for d in range(n)]
    most = functools.reduce(jnp.maximum, parts)
    lse = most + jnp.log(sum(jnp.exp(part - most) for part in parts))
    for r in range(rows_dev):
        for k in range(slots):
            at = at_ref[r * slots + k]
            tile = held[pl.ds(jnp.maximum(at, 0), 1), :] - lse[r : r + 1, :]
            out_ref[r, k : k + 1, :] = jnp.where(at >= 0, tile, jnp.float32(0.0))


def body(n, hidden, head, block_ids, valid_count, beam_order):
    me = lax.axis_index("vocab").astype(jnp.int32)
    rows_dev = hidden.shape[0]
    slots = block_ids.shape[1]
    blocks_dev = head.shape[1] // BLK
    per_owner = rows_dev * slots
    size = CAP + rows_dev
    vmem = pl.BlockSpec(memory_space=pltpu.VMEM)
    smem = pl.BlockSpec(memory_space=pltpu.SMEM)

    apart = (beam_order // rows_dev) ^ me
    row_of = ((apart & 1) * (n // 2) + (apart >> 1)) * rows_dev + beam_order % rows_dev

    ids = block_ids.reshape(n, per_owner)
    device = ids // blocks_dev
    local = ids % blocks_dev
    before = jnp.arange(per_owner)[:, None] > jnp.arange(per_owner)[None, :]
    mine = device == me
    rank = jnp.sum(jnp.where(mine[:, None, :] & before[None], 1, 0), axis=2)
    code = jnp.repeat(row_of.reshape(n, rows_dev), slots, axis=1) + local * (n * rows_dev)
    chosen = mine[:, None, :] & (rank[:, None, :] == jnp.arange(CAP)[None, :, None])
    src = jnp.sum(jnp.where(chosen, code[:, None, :], 0), axis=2).reshape(-1)

    my_ids = lax.dynamic_slice_in_dim(device, me, 1, axis=0)[0]
    my_count = lax.dynamic_slice_in_dim(valid_count, me * rows_dev, rows_dev)
    my_rank = jnp.sum(jnp.where((my_ids[:, None] == my_ids[None, :]) & before, 1, 0), axis=1)
    valid = (jnp.arange(slots)[None, :] < my_count[:, None]).reshape(-1)
    at = jnp.where(valid, (my_ids ^ me) * size + my_rank, -1)

    near = jnp.concatenate([hidden] + [exchange(hidden, n, 2 * t) for t in range(1, n // 2)], axis=0)
    far = exchange(near, n, 1)

    shape = jax.ShapeDtypeStruct((n // NEAR, size, BLK), jnp.float32)
    beams = n * rows_dev
    sent = pl.pallas_call(
        functools.partial(score_kernel, n, rows_dev),
        out_shape=[shape] * NEAR,
        in_specs=[smem, smem, smem, vmem, vmem, vmem],
        out_specs=[vmem] * NEAR,
        scratch_shapes=[pltpu.VMEM((beams, hidden.shape[1]), hidden.dtype), pltpu.VMEM((blocks_dev * beams, BLK), jnp.float32), pltpu.VMEM((beams, BLK), jnp.float32)],
        compiler_params=pltpu.CompilerParams(vmem_limit_bytes=24 * 2**20),
        name="score",
    )(me.reshape(1), src, row_of, near, far, pltpu.with_memory_space_constraint(head, pltpu.VMEM))

    own = [sent[0]] + [exchange(sent[i], n, i) for i in range(1, NEAR)]
    others = [
        exchange(jnp.stack([part[j] for part in own]), n, NEAR * j) for j in range(1, n // NEAR)
    ]
    return pl.pallas_call(
        functools.partial(place_kernel, n, rows_dev, slots),
        out_shape=jax.ShapeDtypeStruct((rows_dev, slots, BLK), jnp.float32),
        in_specs=[smem] + [vmem] * (NEAR + n // NEAR - 1),
        out_specs=vmem,
        scratch_shapes=[pltpu.VMEM((n * size, BLK), jnp.float32)],
        name="place",
    )(at, *own, *others)


def solution(mesh):
    return jax.shard_map(
        functools.partial(body, mesh.shape["vocab"]),
        mesh=mesh,
        in_specs=(P(("grp", "vocab"), None), P(None, "vocab"), P("grp", None), P("grp"), P("grp")),
        out_specs=P(("grp", "vocab"), None, None),
        check_vma=False,
    )
```

time: 168 us -> 46.8 us (0.28)
  blocking collectives: 72 us -> 0 us
  waiting for transfers between devices: 61.2 us -> 11.2 us
  between operations: 13.4 us -> 0.16 us
  starting transfers between devices: 0.01 us -> 13.2 us
  matrix products: 10.5 us -> 0 us
  Pallas kernels: 0 us -> 7.12 us
  local copies, waits for them, and re-layouts: 8.83 us -> 11.3 us
  other arithmetic: 1.4 us -> 3.39 us
    reduce_scatter x1 -> x0, waiting for transfers between devices: 61.2 us -> none  [body(): return lax.psum_scatter(term, 'vocab', scatter_dimension=0, tiled=True)]
    all_gather x1 -> x0, blocking collectives: 33.3 us -> none  [body(): lax.all_gather(hidden, 'vocab', axis=0, tiled=True)]
    pmax x1 -> x0, blocking collectives: 21.5 us -> none  [body(): top = lax.pmax(local_max, 'vocab')]
    psum x1 -> x0, blocking collectives: 17.1 us -> none  [body(): total = lax.psum(jnp.sum(jnp.exp(logits - top[:, None]), axis=1), 'vocab')]
    ppermute x0 -> x8, starting transfers between devices: none -> 13.2 us  [exchange(): return lax.ppermute(x, 'vocab', [(i, i ^ mask) for i in range(n)])]
    ppermute x0 -> x8, waiting for transfers between devices: none -> 11.2 us  [exchange(): return lax.ppermute(x, 'vocab', [(i, i ^ mask) for i in range(n)])]
    dot_general x1 -> x0, matrix products: 10.5 us -> none  [body(): jnp.dot(lax.all_gather(hidden, 'vocab', axis=0, tiled=True), head, prefer...]
    unnamed x7 -> x15, local copies, waits for them, and re-layouts: 0.15 us -> 9.64 us
  transfers between devices with their start and end apart: 1 -> 8, of which waited for: 1 -> 5; matrix products, arithmetic and copies ran while one was open for 0% -> 13% of each run, Pallas kernels for 0% -> 0%
where the time goes in v1:
time: 46.8 us; the launch traced here: 46.4 us
  starting transfers between devices  13.2 us (28%)
  local copies, waits for them, and re-layouts  11.3 us (24%)
  waiting for transfers between devices  11.2 us (24%)
  Pallas kernels  7.12 us (15%)
  other arithmetic  3.39 us (7%)
    ppermute x8, starting transfers between devices, exchange(): return lax.ppermute(x, 'vocab', [(i, i ^ mask) for i in range(n)])  13.2 us
    ppermute x8, waiting for transfers between devices, exchange(): return lax.ppermute(x, 'vocab', [(i, i ^ mask) for i in range(n)])  11.2 us
    unnamed x15, local copies, waits for them, and re-layouts  9.64 us
    pallas_call x1, Pallas kernels, body(): pl.pallas_call(functools.partial(score_kernel, n, rows_dev), out_shape=[s...  5.37 us
    pallas_call x1, Pallas kernels, body(): pl.pallas_call(functools.partial(place_kernel, n, rows_dev, slots), out_s...  1.75 us
  transfers between devices with their start and end apart: 8, of which 5 were waited for; matrix products, arithmetic and copies ran while one was open for 13% of the time, Pallas kernels for 0%

profile of v1, /device:TPU:0, one launch (start us, length us, event | category | flops | bytes accessed | tf_op | source)
XLA Modules:
  0.0 46.4 jit_solution(2449469967503119122)
XLA Ops:
  0.0 3.0 %collective-permute-start = (bf16[8,4096]{1,0:T(8,128)(2,1)}, bf16[8,4096]{1,0:T(8,128)(2,1)S(1)}, u32[]{:S(2)}, u32[]{:S(2)}) collective-permute-start(bf16[8,4096]{1,0:T(8,128)(2,1)} %param.5), channel_id=1, source_target_pairs={{0,2},{1,3},{2,0},{3,1},{4,6},{5,7},{6,4},{7,5},{8,10},{9,11},{10,... | collective-permute-start | bytes 196616 | tf_op jit(solution)/shard_map/ppermute | solution.py:16
  3.0 2.6 %collective-permute-start.1 = (bf16[8,4096]{1,0:T(8,128)(2,1)}, bf16[8,4096]{1,0:T(8,128)(2,1)S(1)}, u32[]{:S(2)}, u32[]{:S(2)}) collective-permute-start(bf16[8,4096]{1,0:T(8,128)(2,1)} %param.5), channel_id=1, source_target_pairs={{0,4},{1,5},{2,6},{3,7},{4,0},{5,1},{6,2},{7,3},{8,12},{9,13},{10,... | collective-permute-start | bytes 196616 | tf_op jit(solution)/shard_map/ppermute | solution.py:16
  5.6 0.0 collective-permute-start.2
  5.6 0.7 %broadcast_remainder_fusion = (s32[64,16]{0,1:T(8,128)S(1)}, s32[64,16]{0,1:T(8,128)S(1)}) fusion(s32[64,16]{0,1:T(8,128)} %param.7), kind=kLoop, calls=%fused_computation.17 | loop fusion | flops 2048 | bytes 12288 | tf_op jit(solution)/shard_map/jit(floor_divide)/rem | solution.py:78
  6.3 0.7 %sign_compare_fusion = pred[64,16]{0,1:T(8,128)(4,1)S(1)} fusion(s32[64,16]{0,1:T(8,128)} %param.7), kind=kLoop, calls=%fused_computation.11 | loop fusion | flops 2048 | bytes 5120 | tf_op jit(solution)/shard_map/jit(floor_divide)/ne | solution.py:78
  7.0 0.8 %constant_dynamic-update-slice_fusion.3 = bf16[32,4096]{1,0:T(8,128)(2,1)S(1)} fusion(bf16[8,4096]{1,0:T(8,128)(2,1)} %param.5), kind=kLoop, calls=%fused_computation.10 | loop fusion | bytes 131072
  7.9 0.1 copy.11
  8.0 0.1 div.26
  8.1 0.1 copy.9
  8.2 0.1 ne.62
  8.2 0.1 copy.10
  8.3 0.1 rem.50
  8.4 0.7 %fusion.3.order_ref = s32[64]{0:T(128)S(1)} fusion(s32[64]{0:T(128)} %param.9, s32[]{:T(128)} %axis_index.12), kind=kLoop, calls=%fused_computation.26 | loop fusion | flops 1664 | bytes 516 | tf_op jit(solution)/shard_map/add | solution.py:75
  9.1 0.1 reshape.72
  9.2 0.1 broadcast_in_dim.50
  9.2 0.1 reshape.73
  9.4 0.2 select_reduce_fusion
  9.6 0.2 select_reduce_fusion.1
  9.8 0.0 collective-permute-done
  9.8 0.7 %collective-permute-done.1 = bf16[8,4096]{1,0:T(8,128)(2,1)S(1)} collective-permute-done((bf16[8,4096]{1,0:T(8,128)(2,1)}, bf16[8,4096]{1,0:T(8,128)(2,1)S(1)}, u32[]{:S(2)}, u32[]{:S(2)}) %collective-permute-start.1) | collective-permute-done | bytes 65568 | tf_op jit(solution)/shard_map/ppermute | solution.py:16
  10.5 1.4 %collective-permute-done.2 = bf16[8,4096]{1,0:T(8,128)(2,1)S(1)} collective-permute-done((bf16[8,4096]{1,0:T(8,128)(2,1)}, bf16[8,4096]{1,0:T(8,128)(2,1)S(1)}, u32[]{:S(2)}, u32[]{:S(2)}) %collective-permute-start.2) | collective-permute-done | bytes 65568 | tf_op jit(solution)/shard_map/ppermute | solution.py:16
  11.9 1.5 %collective-permute-start.3 = (bf16[32,4096]{1,0:T(8,128)(2,1)S(1)}, bf16[32,4096]{1,0:T(8,128)(2,1)S(1)}, u32[]{:S(2)}, u32[]{:S(2)}) collective-permute-start(bf16[32,4096]{1,0:T(8,128)(2,1)S(1)} %constant_dynamic-update-slice_fusion.near_ref), channel_id=1, source_target_pairs={{0,1},{1,0},{2,3},{3,2},{4,5},{5,4},{6,7},{7,6},{8,9},{9,8},{10,11... | collective-permute-start | bytes 786440 | tf_op jit(solution)/shard_map/ppermute | solution.py:16
  13.4 0.1 reshape.74.src_ref
  13.5 0.7 %dynamic_slice.6 = s32[8]{0:T(128)S(1)} dynamic-slice(s32[64]{0:T(128)} %param.8, s32[]{:T(128)S(6)} %select_n.53), dynamic_slice_sizes={8} | dynamic-slice | bytes 68 | tf_op jit(solution)/shard_map/dynamic_slice | solution.py:88
  14.3 0.1 iota_compare_fusion.2
  14.3 4.0 %collective-permute-done.3.far_ref = bf16[32,4096]{1,0:T(8,128)(2,1)S(1)} collective-permute-done((bf16[32,4096]{1,0:T(8,128)(2,1)S(1)}, bf16[32,4096]{1,0:T(8,128)(2,1)S(1)}, u32[]{:S(2)}, u32[]{:S(2)}) %collective-permute-start.3) | collective-permute-done | bytes 262176 | tf_op jit(solution)/shard_map/ppermute | solution.py:16
  18.3 8.2 %copy-done = bf16[4096,3072]{1,0:T(8,128)(2,1)S(1)} copy-done((bf16[4096,3072]{1,0:T(8,128)(2,1)S(1)}, bf16[4096,3072]{1,0:T(8,128)(2,1)}, u32[]{:S(2)}) %copy-start) | copy-done | bytes 25165848
  26.5 5.4 %score.1 = (f32[2,24,128]{2,1,0:T(8,128)S(1)}, f32[2,24,128]{2,1,0:T(8,128)S(1)}, f32[2,24,128]{2,1,0:T(8,128)S(1)}, f32[2,24,128]{2,1,0:T(8,128)S(1)}) custom-call(s32[1]{0:T(128)} %bitcast.1.me_ref, s32[128]{0:T(128)S(1)} %reshape.74.src_ref, s32[64]{0:T(128)S(1)} %fusion.3.order_ref, bf16[32,4096]{1,0:T(8,128)(2,1)S(1)} %constant_dynamic-update-slice_fusion.near_ref, ...), custom_call_target="tpu_custom_call" | custom-call | tf_op jit(solution)/shard_map/score/pallas_call | solution.py:98
  31.9 0.0 copy-start.1
  31.9 1.6 %collective-permute-start.4 = (f32[2,24,128]{2,1,0:T(8,128)S(1)}, f32[2,24,128]{2,1,0:T(8,128)S(1)}, u32[]{:S(2)}, u32[]{:S(2)}) collective-permute-start(f32[2,24,128]{2,1,0:T(8,128)S(1)} %get-tuple-element.10), channel_id=1, source_target_pairs={{0,1},{1,0},{2,3},{3,2},{4,5},{5,4},{6,7},{7,6},{8,9},{9,8},{10,11... | collective-permute-start | bytes 73736 | tf_op jit(solution)/shard_map/ppermute | solution.py:16
  33.5 0.7 %collective-permute-start.5 = (f32[2,24,128]{2,1,0:T(8,128)S(1)}, f32[2,24,128]{2,1,0:T(8,128)S(1)}, u32[]{:S(2)}, u32[]{:S(2)}) collective-permute-start(f32[2,24,128]{2,1,0:T(8,128)S(1)} %get-tuple-element.11), channel_id=1, source_target_pairs={{0,2},{1,3},{2,0},{3,1},{4,6},{5,7},{6,4},{7,5},{8,10},{9,11},{10,... | collective-permute-start | bytes 73736 | tf_op jit(solution)/shard_map/ppermute | solution.py:16
  34.2 1.3 %collective-permute-start.6 = (f32[2,24,128]{2,1,0:T(8,128)S(1)}, f32[2,24,128]{2,1,0:T(8,128)S(1)}, u32[]{:S(2)}, u32[]{:S(2)}) collective-permute-start(f32[2,24,128]{2,1,0:T(8,128)S(1)} %get-tuple-element.12), channel_id=1, source_target_pairs={{0,3},{1,2},{2,1},{3,0},{4,7},{5,6},{6,5},{7,4},{8,11},{9,10},{10,... | collective-permute-start | bytes 73736 | tf_op jit(solution)/shard_map/ppermute | solution.py:16
  35.4 0.2 select_reduce_fusion.2
  35.6 0.1 lt.39
  35.7 3.2 %collective-permute-done.6.refs_3_ = f32[2,24,128]{2,1,0:T(8,128)S(1)} collective-permute-done((f32[2,24,128]{2,1,0:T(8,128)S(1)}, f32[2,24,128]{2,1,0:T(8,128)S(1)}, u32[]{:S(2)}, u32[]{:S(2)}) %collective-permute-start.6) | collective-permute-done | bytes 24608 | tf_op jit(solution)/shard_map/ppermute | solution.py:16
  38.9 0.0 collective-permute-done.5.refs_2_
  38.9 0.0 copy-start.3
  38.9 0.0 collective-permute-done.4.refs_1_
  38.9 0.0 copy-start.2
  39.0 2.6 %collective-permute-start.7 = (f32[4,24,128]{2,1,0:T(8,128)S(1)}, f32[4,24,128]{2,1,0:T(8,128)S(1)}, u32[]{:S(2)}, u32[]{:S(2)}) collective-permute-start(f32[4,24,128]{2,1,0:T(8,128)S(1)} %pad_maximum_fusion), channel_id=1, source_target_pairs={{0,4},{1,5},{2,6},{3,7},{4,0},{5,1},{6,2},{7,3},{8,12},{9,13},{10,... | collective-permute-start | bytes 147464 | tf_op jit(solution)/shard_map/ppermute | solution.py:16
  41.5 0.6 %add_select_fusion.2.at_ref = s32[128]{0:T(128)} fusion(pred[128]{0:T(512)(128)(4,1)S(1)} %lt.39, s32[128]{0:T(128)S(1)} %select_reduce_fusion.2, s32[]{:T(128)} %axis_index.12, s32[8,128]{1,0:T(8,128)S(1)} %get-tuple-element.14, s32[]{:T(128)S(6)} %select_n.55), kind=kLoop, calls=%fused_computation.27 | loop fusion | flops 512 | bytes 1672 | tf_op jit(solution)/shard_map/jit(_where)/select_n | solution.py:91
  42.1 1.9 %collective-permute-done.7.refs_4_ = f32[4,24,128]{2,1,0:T(8,128)S(1)} collective-permute-done((f32[4,24,128]{2,1,0:T(8,128)S(1)}, f32[4,24,128]{2,1,0:T(8,128)S(1)}, u32[]{:S(2)}, u32[]{:S(2)}) %collective-permute-start.7) | collective-permute-done | bytes 49184 | tf_op jit(solution)/shard_map/ppermute | solution.py:16
  44.0 0.0 copy-done.1
  44.0 0.0 copy-done.3
  44.0 0.0 copy-done.2
  44.0 0.0 copy-start.5
  44.1 0.6 %copy-done.5 = f32[4,24,128]{2,1,0:T(8,128)} copy-done((f32[4,24,128]{2,1,0:T(8,128)}, f32[4,24,128]{2,1,0:T(8,128)S(1)}, u32[]{:S(2)}) %copy-start.5) | copy-done | bytes 49176
  44.7 1.8 %place.1 = f32[8,16,128]{2,1,0:T(8,128)} custom-call(s32[128]{0:T(128)} %add_select_fusion.2.at_ref, f32[2,24,128]{2,1,0:T(8,128)} %copy-done.1, f32[2,24,128]{2,1,0:T(8,128)} %copy-done.2, f32[2,24,128]{2,1,0:T(8,128)} %copy-done.3, f32[2,24,128]{2,1,0:T(8,128)} %copy-done.4, f32[4,24,128]{2,1,0:T(8,128)} %copy-done.5), custom_call_target="tpu_custom_call" | custom-call | tf_op jit(solution)/shard_map/place/pallas_call | solution.py:112
  (15 shorter events, 0.1 us)
Async XLA Ops:
  0.0 9.8 %collective-permute-start = (bf16[8,4096]{1,0:T(8,128)(2,1)}, bf16[8,4096]{1,0:T(8,128)(2,1)S(1)}, u32[]{:S(2)}, u32[]{:S(2)}) collective-permute-start(bf16[8,4096]{1,0:T(8,128)(2,1)} %param.5), channel_id=1, source_target_pairs={{0,2},{1,3},{2,0},{3,1},{4,6},{5,7},{6,4},{7,5},{8,10},{9,11},{10,... | collective-permute-start | bytes 196616 | tf_op jit(solution)/shard_map/ppermute | solution.py:16
  3.0 7.5 %collective-permute-start.1 = (bf16[8,4096]{1,0:T(8,128)(2,1)}, bf16[8,4096]{1,0:T(8,128)(2,1)S(1)}, u32[]{:S(2)}, u32[]{:S(2)}) collective-permute-start(bf16[8,4096]{1,0:T(8,128)(2,1)} %param.5), channel_id=1, source_target_pairs={{0,4},{1,5},{2,6},{3,7},{4,0},{5,1},{6,2},{7,3},{8,12},{9,13},{10,... | collective-permute-start | bytes 196616 | tf_op jit(solution)/shard_map/ppermute | solution.py:16
  5.6 6.3 %collective-permute-start.2 = (bf16[8,4096]{1,0:T(8,128)(2,1)}, bf16[8,4096]{1,0:T(8,128)(2,1)S(1)}, u32[]{:S(2)}, u32[]{:S(2)}) collective-permute-start(bf16[8,4096]{1,0:T(8,128)(2,1)} %param.5), channel_id=1, source_target_pairs={{0,6},{1,7},{2,4},{3,5},{4,2},{5,3},{6,0},{7,1},{8,14},{9,15},{10,... | collective-permute-start | bytes 196616 | tf_op jit(solution)/shard_map/ppermute | solution.py:16
  11.9 6.4 %collective-permute-start.3 = (bf16[32,4096]{1,0:T(8,128)(2,1)S(1)}, bf16[32,4096]{1,0:T(8,128)(2,1)S(1)}, u32[]{:S(2)}, u32[]{:S(2)}) collective-permute-start(bf16[32,4096]{1,0:T(8,128)(2,1)S(1)} %constant_dynamic-update-slice_fusion.near_ref), channel_id=1, source_target_pairs={{0,1},{1,0},{2,3},{3,2},{4,5},{5,4},{6,7},{7,6},{8,9},{9,8},{10,11... | collective-permute-start | bytes 786440 | tf_op jit(solution)/shard_map/ppermute | solution.py:16
  18.3 8.2 %copy-start = (bf16[4096,3072]{1,0:T(8,128)(2,1)S(1)}, bf16[4096,3072]{1,0:T(8,128)(2,1)}, u32[]{:S(2)}) copy-start(bf16[4096,3072]{1,0:T(8,128)(2,1)} %head_ref.1) | copy-start | bytes 75497472
  31.9 12.2 %copy-start.1 = (f32[2,24,128]{2,1,0:T(8,128)}, f32[2,24,128]{2,1,0:T(8,128)S(1)}, u32[]{:S(2)}) copy-start(f32[2,24,128]{2,1,0:T(8,128)S(1)} %get-tuple-element.9.refs_0_) | copy-start | bytes 73732
  31.9 7.0 %collective-permute-start.4 = (f32[2,24,128]{2,1,0:T(8,128)S(1)}, f32[2,24,128]{2,1,0:T(8,128)S(1)}, u32[]{:S(2)}, u32[]{:S(2)}) collective-permute-start(f32[2,24,128]{2,1,0:T(8,128)S(1)} %get-tuple-element.10), channel_id=1, source_target_pairs={{0,1},{1,0},{2,3},{3,2},{4,5},{5,4},{6,7},{7,6},{8,9},{9,8},{10,11... | collective-permute-start | bytes 73736 | tf_op jit(solution)/shard_map/ppermute | solution.py:16
  33.5 5.4 %collective-permute-start.5 = (f32[2,24,128]{2,1,0:T(8,128)S(1)}, f32[2,24,128]{2,1,0:T(8,128)S(1)}, u32[]{:S(2)}, u32[]{:S(2)}) collective-permute-start(f32[2,24,128]{2,1,0:T(8,128)S(1)} %get-tuple-element.11), channel_id=1, source_target_pairs={{0,2},{1,3},{2,0},{3,1},{4,6},{5,7},{6,4},{7,5},{8,10},{9,11},{10,... | collective-permute-start | bytes 73736 | tf_op jit(solution)/shard_map/ppermute | solution.py:16
  34.2 4.7 %collective-permute-start.6 = (f32[2,24,128]{2,1,0:T(8,128)S(1)}, f32[2,24,128]{2,1,0:T(8,128)S(1)}, u32[]{:S(2)}, u32[]{:S(2)}) collective-permute-start(f32[2,24,128]{2,1,0:T(8,128)S(1)} %get-tuple-element.12), channel_id=1, source_target_pairs={{0,3},{1,2},{2,1},{3,0},{4,7},{5,6},{6,5},{7,4},{8,11},{9,10},{10,... | collective-permute-start | bytes 73736 | tf_op jit(solution)/shard_map/ppermute | solution.py:16
  38.9 5.1 %copy-start.4 = (f32[2,24,128]{2,1,0:T(8,128)}, f32[2,24,128]{2,1,0:T(8,128)S(1)}, u32[]{:S(2)}) copy-start(f32[2,24,128]{2,1,0:T(8,128)S(1)} %collective-permute-done.6.refs_3_) | copy-start | bytes 73732
  38.9 5.1 %copy-start.3 = (f32[2,24,128]{2,1,0:T(8,128)}, f32[2,24,128]{2,1,0:T(8,128)S(1)}, u32[]{:S(2)}) copy-start(f32[2,24,128]{2,1,0:T(8,128)S(1)} %collective-permute-done.5.refs_2_) | copy-start | bytes 73732
  38.9 5.1 %copy-start.2 = (f32[2,24,128]{2,1,0:T(8,128)}, f32[2,24,128]{2,1,0:T(8,128)S(1)}, u32[]{:S(2)}) copy-start(f32[2,24,128]{2,1,0:T(8,128)S(1)} %collective-permute-done.4.refs_1_) | copy-start | bytes 73732
  39.0 5.1 %collective-permute-start.7 = (f32[4,24,128]{2,1,0:T(8,128)S(1)}, f32[4,24,128]{2,1,0:T(8,128)S(1)}, u32[]{:S(2)}, u32[]{:S(2)}) collective-permute-start(f32[4,24,128]{2,1,0:T(8,128)S(1)} %pad_maximum_fusion), channel_id=1, source_target_pairs={{0,4},{1,5},{2,6},{3,7},{4,0},{5,1},{6,2},{7,3},{8,12},{9,13},{10,... | collective-permute-start | bytes 147464 | tf_op jit(solution)/shard_map/ppermute | solution.py:16
  44.0 0.6 %copy-start.5 = (f32[4,24,128]{2,1,0:T(8,128)}, f32[4,24,128]{2,1,0:T(8,128)S(1)}, u32[]{:S(2)}) copy-start(f32[4,24,128]{2,1,0:T(8,128)S(1)} %collective-permute-done.7.refs_4_) | copy-start | bytes 147460

commit v2 on v1

v2 whole, which is shorter than its diff:
```python
import functools

import jax
import jax.numpy as jnp
from jax import lax
from jax.experimental import pallas as pl
from jax.experimental.pallas import tpu as pltpu
from jax.sharding import PartitionSpec as P

BLK = 128
CAP = 16
NEAR = 4


def exchange(x, n, mask):
    return lax.ppermute(x, "vocab", [(i, i ^ mask) for i in range(n)])


def split(n, rows_dev):
    beams = n * rows_dev
    at = lax.broadcasted_iota(jnp.int32, (beams, beams), 0)
    to = lax.broadcasted_iota(jnp.int32, (beams, beams), 1)
    shift = rows_dev.bit_length() - 1
    same = (at >> shift) == (to >> shift)
    return same.astype(jnp.bfloat16), (same & (at < to)).astype(jnp.bfloat16)


def counts(a, b):
    return jnp.dot(a, b, preferred_element_type=jnp.float32)


def fetch_kernel(
    n,
    rows_dev,
    blocks_dev,
    me_ref,
    ids_hbm,
    valid_hbm,
    order_hbm,
    head_hbm,
    after,
    src_ref,
    rows_ref,
    at_ref,
    held_ref,
    ids_ref,
    valid_ref,
    order_ref,
    sems,
):
    copies = [
        pltpu.make_async_copy(ids_hbm, ids_ref, sems.at[0]),
        pltpu.make_async_copy(valid_hbm, valid_ref, sems.at[1]),
        pltpu.make_async_copy(order_hbm, order_ref, sems.at[2]),
        pltpu.make_async_copy(head_hbm.at[:, : held_ref.shape[1]], held_ref, sems.at[3]),
    ]
    for copy in copies:
        copy.start()
    for copy in copies[:3]:
        copy.wait()
    me = me_ref[0]
    slots, beams = ids_ref.shape
    shift = rows_dev.bit_length() - 1
    apart = (order_ref[...] >> shift) ^ me
    row_of = ((apart & (NEAR - 1)) * (n // NEAR) + (apart >> (NEAR.bit_length() - 1))) * rows_dev
    row_of = row_of + (order_ref[...] & (rows_dev - 1))
    rows_ref[...] = row_of

    ids = ids_ref[...]
    same, earlier = split(n, rows_dev)
    k_at = lax.broadcasted_iota(jnp.int32, (slots, slots), 0)
    k_to = lax.broadcasted_iota(jnp.int32, (slots, slots), 1)
    below = (k_to < k_at).astype(jnp.bfloat16)

    def rank(on):
        ones = jnp.where(on, 1.0, 0.0).astype(jnp.bfloat16)
        return (counts(ones, earlier) + counts(below, counts(ones, same).astype(jnp.bfloat16))).astype(jnp.int32)

    at = jnp.zeros((slots, beams), jnp.int32)
    for d in range(n):
        on = (ids >= d * blocks_dev) & (ids < (d + 1) * blocks_dev)
        at = jnp.where(on, (me ^ d) * (CAP + rows_dev) + rank(on), at)
    k_index = lax.broadcasted_iota(jnp.int32, (slots, beams), 0)
    at_ref[...] = jnp.where(k_index < valid_ref[...], at, -1)

    first = me * blocks_dev
    mine = (ids >= first) & (ids < first + blocks_dev)
    my_rank = jnp.where(mine, rank(mine), -1)
    local = ids - first
    owner = (
        (lax.broadcasted_iota(jnp.int32, (beams, n), 0) >> shift) == lax.broadcasted_iota(jnp.int32, (beams, n), 1)
    ).astype(jnp.bfloat16)
    rows = jnp.broadcast_to(row_of, (slots, beams))

    def gathered(value):
        picked = [jnp.sum(jnp.where(my_rank == j, value, 0), axis=0, keepdims=True) for j in range(CAP)]
        table = jnp.concatenate(picked, axis=0).astype(jnp.float32).astype(jnp.bfloat16)
        return counts(table, owner).astype(jnp.int32)

    src_ref[...] = gathered(local) * beams + gathered(rows)
    copies[3].wait()


def score_kernel(n, rows_dev, me_ref, src_vmem, rows_vmem, x_ref, held_ref, head_hbm, *refs):
    outs, (rest, logits, stats, src_ref, rows_ref, sems, index_sems) = refs[:NEAR], refs[NEAR:]
    beams = x_ref.shape[0]
    held = held_ref.shape[1]
    blocks = head_hbm.shape[1] // BLK
    step = rest.shape[2]
    chunks = [
        pltpu.make_async_copy(head_hbm.at[:, held + c * step : held + (c + 1) * step], rest.at[c], sems.at[c])
        for c in range(rest.shape[0])
    ]
    copies = [
        pltpu.make_async_copy(src_vmem, src_ref, index_sems.at[0]),
        pltpu.make_async_copy(rows_vmem, rows_ref, index_sems.at[1]),
    ]
    for copy in chunks + copies:
        copy.start()

    def multiply(columns, base):
        product = jnp.dot(x_ref[...], columns, preferred_element_type=jnp.float32)
        for i in range(step // BLK):
            logits[(base + i) * beams : (base + i + 1) * beams, :] = product[:, i * BLK : (i + 1) * BLK]

    for c in range(held // step):
        multiply(held_ref[:, c * step : (c + 1) * step], c * (step // BLK))
    for c, chunk in enumerate(chunks):
        chunk.wait()
        multiply(rest[c], (held + c * step) // BLK)
    most = functools.reduce(jnp.maximum, [logits[j * beams : (j + 1) * beams, :] for j in range(blocks)])
    most = jnp.max(most, axis=1, keepdims=True)
    total = sum(jnp.exp(logits[j * beams : (j + 1) * beams, :] - most) for j in range(blocks))
    lse = most + jnp.log(jnp.sum(total, axis=1, keepdims=True))
    stats[...] = jnp.broadcast_to(lse, (beams, BLK))
    for copy in copies:
        copy.wait()
    me = me_ref[0]
    for near in range(NEAR):
        for far in range(n // NEAR):
            owner = me ^ (far * NEAR + near)
            for k in range(CAP):
                outs[near][far, k : k + 1, :] = logits[pl.ds(src_ref[k, owner], 1), :]
            for i in range(rows_dev):
                outs[near][far, CAP + i : CAP + i + 1, :] = stats[pl.ds(rows_ref[0, owner * rows_dev + i], 1), :]


def place_kernel(n, rows_dev, slots, me_ref, at_vmem, *refs):
    own, others = refs[:NEAR], refs[NEAR : NEAR + n // NEAR - 1]
    out_ref, held, at_ref, sem = refs[-4:]
    copy = pltpu.make_async_copy(at_vmem, at_ref, sem)
    copy.start()
    size = CAP + rows_dev
    for near in range(NEAR):
        held[near * size : (near + 1) * size, :] = own[near][0]
        for far in range(1, n // NEAR):
            base = (far * NEAR + near) * size
            held[base : base + size, :] = others[far - 1][near]
    parts = [held[d * size + CAP : (d + 1) * size, :] for d in range(n)]
    most = functools.reduce(jnp.maximum, parts)
    lse = most + jnp.log(sum(jnp.exp(part - most) for part in parts))
    copy.wait()
    first = me_ref[0] * rows_dev
    for r in range(rows_dev):
        for k in range(slots):
            at = at_ref[k, first + r]
            tile = held[pl.ds(jnp.maximum(at, 0), 1), :] - lse[r : r + 1, :]
            out_ref[r, k : k + 1, :] = jnp.where(at >= 0, tile, jnp.float32(0.0))


def in_vmem(x):
    return pltpu.with_memory_space_constraint(x, pltpu.VMEM)


def in_hbm(x):
    return pltpu.with_memory_space_constraint(x, pltpu.HBM)


def body(n, hidden, head, block_ids, valid_count, beam_order):
    me = lax.axis_index("vocab").astype(jnp.int32).reshape(1)
    rows_dev = hidden.shape[0]
    beams, slots = block_ids.shape
    blocks_dev = head.shape[1] // BLK
    size = CAP + rows_dev
    fars = n // NEAR
    depth = head.shape[0]
    held = blocks_dev // 2 * BLK
    step = 4 * BLK if held % (4 * BLK) == 0 and (head.shape[1] - held) % (4 * BLK) == 0 else BLK
    vmem = pl.BlockSpec(memory_space=pltpu.VMEM)
    smem = pl.BlockSpec(memory_space=pltpu.SMEM)
    hbm = pl.BlockSpec(memory_space=pltpu.HBM)
    anywhere = pl.BlockSpec(memory_space=pl.ANY)

    far = [exchange(hidden, n, NEAR * f) for f in range(1, fars)]
    near = [exchange(hidden, n, i) for i in range(1, NEAR)]
    far = far[0] if fars == 2 else jnp.concatenate(far, axis=0)
    src, row_of, at, first = pl.pallas_call(
        functools.partial(fetch_kernel, n, rows_dev, blocks_dev),
        out_shape=[
            jax.ShapeDtypeStruct((CAP, n), jnp.int32),
            jax.ShapeDtypeStruct((1, beams), jnp.int32),
            jax.ShapeDtypeStruct((slots, beams), jnp.int32),
            pltpu.VMEM((depth, held), head.dtype),
        ],
        in_specs=[smem, hbm, hbm, hbm, hbm, anywhere],
        out_specs=[vmem] * 4,
        scratch_shapes=[
            pltpu.VMEM((slots, beams), jnp.int32),
            pltpu.VMEM((1, beams), jnp.int32),
            pltpu.VMEM((1, beams), jnp.int32),
            pltpu.SemaphoreType.DMA((4,)),
        ],
        cost_estimate=pl.CostEstimate(flops=0, bytes_accessed=2 * depth * held, transcendentals=0),
        compiler_params=pltpu.CompilerParams(vmem_limit_bytes=4 * 2**20),
        name="fetch",
    )(
        me,
        in_hbm(block_ids.T),
        in_hbm(valid_count.reshape(1, beams)),
        in_hbm(beam_order.reshape(1, beams)),
        in_hbm(head),
        far,
    )

    passed = [exchange(far, n, i) for i in range(1, NEAR)]
    x = jnp.concatenate([hidden, far] + [part for pair in zip(near, passed) for part in pair], axis=0)

    shape = jax.ShapeDtypeStruct((fars, size, BLK), jnp.float32)
    sent = pl.pallas_call(
        functools.partial(score_kernel, n, rows_dev),
        out_shape=[shape] * NEAR,
        in_specs=[smem, vmem, vmem, vmem, vmem, hbm],
        out_specs=[vmem] * NEAR,
        scratch_shapes=[
            pltpu.VMEM(((head.shape[1] - held) // step, depth, step), head.dtype),
            pltpu.VMEM((blocks_dev * beams, BLK), jnp.float32),
            pltpu.VMEM((beams, BLK), jnp.float32),
            pltpu.SMEM((CAP, n), jnp.int32),
            pltpu.SMEM((1, beams), jnp.int32),
            pltpu.SemaphoreType.DMA(((head.shape[1] - held) // step,)),
            pltpu.SemaphoreType.DMA((2,)),
        ],
        compiler_params=pltpu.CompilerParams(vmem_limit_bytes=24 * 2**20),
        name="score",
    )(me, in_vmem(src), in_vmem(row_of), in_vmem(x), in_vmem(first), in_hbm(head))

    own = [sent[0]] + [exchange(sent[i], n, i) for i in range(1, NEAR)]
    others = [exchange(jnp.stack([part[j] for part in own]), n, NEAR * j) for j in range(1, fars)]
    return pl.pallas_call(
        functools.partial(place_kernel, n, rows_dev, slots),
        out_shape=jax.ShapeDtypeStruct((rows_dev, slots, BLK), jnp.float32),
        in_specs=[smem, vmem] + [vmem] * (NEAR + fars - 1),
        out_specs=vmem,
        scratch_shapes=[
            pltpu.VMEM((n * size, BLK), jnp.float32),
            pltpu.SMEM((slots, beams), jnp.int32),
            pltpu.SemaphoreType.DMA,
        ],
        name="place",
    )(me, in_vmem(at), *map(in_vmem, own), *map(in_vmem, others))


def solution(mesh):
    return jax.shard_map(
        functools.partial(body, mesh.shape["vocab"]),
        mesh=mesh,
        in_specs=(P(("grp", "vocab"), None), P(None, "vocab"), P("grp", None), P("grp"), P("grp")),
        out_specs=P(("grp", "vocab"), None, None),
        check_vma=False,
    )
```

time: 46.8 us -> 37.6 us (0.80)
  local copies, waits for them, and re-layouts: 11.3 us -> 0.93 us
  Pallas kernels: 7.12 us -> 12.3 us
  waiting for transfers between devices: 11.2 us -> 6.99 us
  starting transfers between devices: 13.2 us -> 17 us
  other arithmetic: 3.39 us -> 0.01 us
    unnamed x15 -> x7, local copies, waits for them, and re-layouts: 9.64 us -> 0.92 us
    pallas_call x0 -> x1, Pallas kernels: none -> 4.66 us  [body(): pl.pallas_call(functools.partial(fetch_kernel, n, rows_dev, blocks_dev),...]
    ppermute x8 -> x11, waiting for transfers between devices: 11.2 us -> 6.99 us  [exchange(): return lax.ppermute(x, 'vocab', [(i, i ^ mask) for i in range(n)])]
    ppermute x8 -> x11, starting transfers between devices: 13.2 us -> 17 us  [exchange(): return lax.ppermute(x, 'vocab', [(i, i ^ mask) for i in range(n)])]
    dynamic_slice x1 -> x0, local copies, waits for them, and re-layouts: 0.73 us -> none  [body(): my_count = lax.dynamic_slice_in_dim(valid_count, me * rows_dev, rows_dev)]
    rem x1 -> x0, other arithmetic: 0.71 us -> none  [body(): device = ids // blocks_dev]
    ne x1 -> x0, other arithmetic: 0.7 us -> none  [body(): device = ids // blocks_dev]
    pallas_call x1, Pallas kernels: 5.37 us -> 6.07 us  [body(): pl.pallas_call(functools.partial(score_kernel, n, rows_dev), out_shape=[s...]
  transfers between devices with their start and end apart: 8 -> 11, of which waited for: 5 -> 5; matrix products, arithmetic and copies ran while one was open for 13% -> 2% of each run, Pallas kernels for 0% -> 12%
where the time goes in v2:
time: 37.6 us; the launch traced here: 37.4 us
  starting transfers between devices  17 us (45%)
  Pallas kernels  12.3 us (33%)
  waiting for transfers between devices  6.99 us (19%)
  local copies, waits for them, and re-layouts  0.93 us (2%)
    ppermute x11, starting transfers between devices, exchange(): return lax.ppermute(x, 'vocab', [(i, i ^ mask) for i in range(n)])  17 us
    ppermute x11, waiting for transfers between devices, exchange(): return lax.ppermute(x, 'vocab', [(i, i ^ mask) for i in range(n)])  6.99 us
    pallas_call x1, Pallas kernels, body(): pl.pallas_call(functools.partial(score_kernel, n, rows_dev), out_shape=[s...  6.07 us
    pallas_call x1, Pallas kernels, body(): pl.pallas_call(functools.partial(fetch_kernel, n, rows_dev, blocks_dev),...  4.66 us
    pallas_call x1, Pallas kernels, body(): pl.pallas_call(functools.partial(place_kernel, n, rows_dev, slots), out_s...  1.61 us
    unnamed x7, local copies, waits for them, and re-layouts  0.92 us
  transfers between devices with their start and end apart: 11, of which 5 were waited for; matrix products, arithmetic and copies ran while one was open for 2% of the time, Pallas kernels for 12%

profile of v2, /device:TPU:0, one launch (start us, length us, event | category | flops | bytes accessed | tf_op | source)
XLA Modules:
  0.0 37.4 jit_solution(13389174538184701167)
XLA Ops:
  0.0 3.0 %collective-permute-start.3 = (bf16[8,4096]{1,0:T(8,128)(2,1)}, bf16[8,4096]{1,0:T(8,128)(2,1)S(1)}, u32[]{:S(2)}, u32[]{:S(2)}) collective-permute-start(bf16[8,4096]{1,0:T(8,128)(2,1)} %param.5), channel_id=1, source_target_pairs={{0,2},{1,3},{2,0},{3,1},{4,6},{5,7},{6,4},{7,5},{8,10},{9,11},{10,... | collective-permute-start | bytes 196616 | tf_op jit(solution)/shard_map/ppermute | solution.py:16
  3.0 1.5 %collective-permute-start.1 = (bf16[8,4096]{1,0:T(8,128)(2,1)}, bf16[8,4096]{1,0:T(8,128)(2,1)S(1)}, u32[]{:S(2)}, u32[]{:S(2)}) collective-permute-start(bf16[8,4096]{1,0:T(8,128)(2,1)} %param.5), channel_id=1, source_target_pairs={{0,1},{1,0},{2,3},{3,2},{4,5},{5,4},{6,7},{7,6},{8,9},{9,8},{10,11... | collective-permute-start | bytes 196616 | tf_op jit(solution)/shard_map/ppermute | solution.py:16
  4.5 2.6 %collective-permute-start = (bf16[8,4096]{1,0:T(8,128)(2,1)}, bf16[8,4096]{1,0:T(8,128)(2,1)S(1)}, u32[]{:S(2)}, u32[]{:S(2)}) collective-permute-start(bf16[8,4096]{1,0:T(8,128)(2,1)} %param.5), channel_id=1, source_target_pairs={{0,4},{1,5},{2,6},{3,7},{4,0},{5,1},{6,2},{7,3},{8,12},{9,13},{10,... | collective-permute-start | bytes 196616 | tf_op jit(solution)/shard_map/ppermute | solution.py:16
  7.1 0.4 %collective-permute-start.5 = (bf16[8,4096]{1,0:T(8,128)(2,1)}, bf16[8,4096]{1,0:T(8,128)(2,1)S(1)}, u32[]{:S(2)}, u32[]{:S(2)}) collective-permute-start(bf16[8,4096]{1,0:T(8,128)(2,1)} %param.5), channel_id=1, source_target_pairs={{0,3},{1,2},{2,1},{3,0},{4,7},{5,6},{6,5},{7,4},{8,11},{9,10},{10,... | collective-permute-start | bytes 196616 | tf_op jit(solution)/shard_map/ppermute | solution.py:16
  7.5 0.9 %constant_dynamic-update-slice_fusion.7 = bf16[64,4096]{1,0:T(8,128)(2,1)S(1)} fusion(bf16[8,4096]{1,0:T(8,128)(2,1)} %param.5), kind=kLoop, calls=%fused_computation.8 | loop fusion | bytes 131072
  8.4 2.2 %collective-permute-done.after = bf16[8,4096]{1,0:T(8,128)(2,1)S(1)} collective-permute-done((bf16[8,4096]{1,0:T(8,128)(2,1)}, bf16[8,4096]{1,0:T(8,128)(2,1)S(1)}, u32[]{:S(2)}, u32[]{:S(2)}) %collective-permute-start) | collective-permute-done | bytes 65568 | tf_op jit(solution)/shard_map/ppermute | solution.py:16
  10.6 0.3 collective-permute-start.6
  10.9 1.8 %collective-permute-start.4 = (bf16[8,4096]{1,0:T(8,128)(2,1)S(1)}, bf16[8,4096]{1,0:T(8,128)(2,1)S(1)}, u32[]{:S(2)}, u32[]{:S(2)}) collective-permute-start(bf16[8,4096]{1,0:T(8,128)(2,1)S(1)} %collective-permute-done.after), channel_id=1, source_target_pairs={{0,2},{1,3},{2,0},{3,1},{4,6},{5,7},{6,4},{7,5},{8,10},{9,11},{10,... | collective-permute-start | bytes 196616 | tf_op jit(solution)/shard_map/ppermute | solution.py:16
  12.7 0.0 collective-permute-done.1
  12.7 1.5 %collective-permute-start.2 = (bf16[8,4096]{1,0:T(8,128)(2,1)S(1)}, bf16[8,4096]{1,0:T(8,128)(2,1)S(1)}, u32[]{:S(2)}, u32[]{:S(2)}) collective-permute-start(bf16[8,4096]{1,0:T(8,128)(2,1)S(1)} %collective-permute-done.after), channel_id=1, source_target_pairs={{0,1},{1,0},{2,3},{3,2},{4,5},{5,4},{6,7},{7,6},{8,9},{9,8},{10,11... | collective-permute-start | bytes 196616 | tf_op jit(solution)/shard_map/ppermute | solution.py:16
  14.2 4.7 %fetch.1 = (s32[16,8]{1,0:T(8,128)S(1)}, s32[1,64]{1,0:T(1,128)S(1)}, s32[16,64]{1,0:T(8,128)S(1)}, bf16[4096,1536]{1,0:T(8,128)(2,1)S(1)}) custom-call(s32[1]{0:T(128)} %bitcast.me_ref, s32[16,64]{1,0:T(8,128)} %bitcast.4, s32[1,64]{1,0:T(1,128)} %bitcast.5, s32[1,64]{1,0:T(1,128)} %bitcast.6, bf16[4096,3072]{1,0:T(8,128)(2,1)} %head_hbm.3, ...), custom_call_target="tpu_custom_call" | custom-call | bytes 12582912 | tf_op jit(solution)/shard_map/fetch/pallas_call | solution.py:197
  18.8 0.0 collective-permute-done.2
  18.9 0.0 collective-permute-done.3
  18.9 0.0 collective-permute-done.4
  18.9 0.0 collective-permute-done.5
  18.9 0.0 collective-permute-done.6
  19.0 6.1 %score.1 = (f32[2,24,128]{2,1,0:T(8,128)S(1)}, f32[2,24,128]{2,1,0:T(8,128)S(1)}, f32[2,24,128]{2,1,0:T(8,128)S(1)}, f32[2,24,128]{2,1,0:T(8,128)S(1)}) custom-call(s32[1]{0:T(128)} %bitcast.me_ref, s32[16,8]{1,0:T(8,128)S(1)} %get-tuple-element.14.src_vmem, s32[1,64]{1,0:T(1,128)S(1)} %get-tuple-element.15.rows_vmem, ...), custom_call_target="tpu_custom_call" | custom-call | tf_op jit(solution)/shard_map/score/pallas_call | solution.py:229
  25.0 0.7 %collective-permute-start.7 = (f32[2,24,128]{2,1,0:T(8,128)S(1)}, f32[2,24,128]{2,1,0:T(8,128)S(1)}, u32[]{:S(2)}, u32[]{:S(2)}) collective-permute-start(f32[2,24,128]{2,1,0:T(8,128)S(1)} %get-tuple-element.18), channel_id=1, source_target_pairs={{0,1},{1,0},{2,3},{3,2},{4,5},{5,4},{6,7},{7,6},{8,9},{9,8},{10,11... | collective-permute-start | bytes 73736 | tf_op jit(solution)/shard_map/ppermute | solution.py:16
  25.7 0.3 collective-permute-start.8
  26.0 2.6 %collective-permute-start.9 = (f32[2,24,128]{2,1,0:T(8,128)S(1)}, f32[2,24,128]{2,1,0:T(8,128)S(1)}, u32[]{:S(2)}, u32[]{:S(2)}) collective-permute-start(f32[2,24,128]{2,1,0:T(8,128)S(1)} %get-tuple-element.20), channel_id=1, source_target_pairs={{0,3},{1,2},{2,1},{3,0},{4,7},{5,6},{6,5},{7,4},{8,11},{9,10},{10,... | collective-permute-start | bytes 73736 | tf_op jit(solution)/shard_map/ppermute | solution.py:16
  28.6 0.3 collective-permute-done.7.refs_1_
  28.9 0.6 %collective-permute-done.8.refs_2_ = f32[2,24,128]{2,1,0:T(8,128)S(1)} collective-permute-done((f32[2,24,128]{2,1,0:T(8,128)S(1)}, f32[2,24,128]{2,1,0:T(8,128)S(1)}, u32[]{:S(2)}, u32[]{:S(2)}) %collective-permute-start.8) | collective-permute-done | bytes 24608 | tf_op jit(solution)/shard_map/ppermute | solution.py:16
  29.6 1.2 %collective-permute-done.9.refs_3_ = f32[2,24,128]{2,1,0:T(8,128)S(1)} collective-permute-done((f32[2,24,128]{2,1,0:T(8,128)S(1)}, f32[2,24,128]{2,1,0:T(8,128)S(1)}, u32[]{:S(2)}, u32[]{:S(2)}) %collective-permute-start.9) | collective-permute-done | bytes 24608 | tf_op jit(solution)/shard_map/ppermute | solution.py:16
  30.7 2.4 %collective-permute-start.10 = (f32[4,24,128]{2,1,0:T(8,128)S(1)}, f32[4,24,128]{2,1,0:T(8,128)S(1)}, u32[]{:S(2)}, u32[]{:S(2)}) collective-permute-start(f32[4,24,128]{2,1,0:T(8,128)S(1)} %pad_maximum_fusion), channel_id=1, source_target_pairs={{0,4},{1,5},{2,6},{3,7},{4,0},{5,1},{6,2},{7,3},{8,12},{9,13},{10,... | collective-permute-start | bytes 147464 | tf_op jit(solution)/shard_map/ppermute | solution.py:16
  33.2 2.6 %collective-permute-done.10.refs_4_ = f32[4,24,128]{2,1,0:T(8,128)S(1)} collective-permute-done((f32[4,24,128]{2,1,0:T(8,128)S(1)}, f32[4,24,128]{2,1,0:T(8,128)S(1)}, u32[]{:S(2)}, u32[]{:S(2)}) %collective-permute-start.10) | collective-permute-done | bytes 49184 | tf_op jit(solution)/shard_map/ppermute | solution.py:16
  35.8 1.6 %place.1 = f32[8,16,128]{2,1,0:T(8,128)} custom-call(s32[1]{0:T(128)} %bitcast.me_ref, s32[16,64]{1,0:T(8,128)S(1)} %get-tuple-element.13.at_vmem, f32[2,24,128]{2,1,0:T(8,128)S(1)} %get-tuple-element.17.refs_0_, f32[2,24,128]{2,1,0:T(8,128)S(1)} %collective-permute-done.7.refs_1_, f32[2,24,128]{2,1,0:T(8,128)S(1)} %collective-permute-done.8.refs_2_, ...), custom_call_target="tpu_custom_call" | custom-call | tf_op jit(solution)/shard_map/place/pallas_call | solution.py:249
  (12 shorter events, 0.1 us)
Async XLA Ops:
  0.0 18.9 %collective-permute-start.3 = (bf16[8,4096]{1,0:T(8,128)(2,1)}, bf16[8,4096]{1,0:T(8,128)(2,1)S(1)}, u32[]{:S(2)}, u32[]{:S(2)}) collective-permute-start(bf16[8,4096]{1,0:T(8,128)(2,1)} %param.5), channel_id=1, source_target_pairs={{0,2},{1,3},{2,0},{3,1},{4,6},{5,7},{6,4},{7,5},{8,10},{9,11},{10,... | collective-permute-start | bytes 196616 | tf_op jit(solution)/shard_map/ppermute | solution.py:16
  3.0 9.7 %collective-permute-start.1 = (bf16[8,4096]{1,0:T(8,128)(2,1)}, bf16[8,4096]{1,0:T(8,128)(2,1)S(1)}, u32[]{:S(2)}, u32[]{:S(2)}) collective-permute-start(bf16[8,4096]{1,0:T(8,128)(2,1)} %param.5), channel_id=1, source_target_pairs={{0,1},{1,0},{2,3},{3,2},{4,5},{5,4},{6,7},{7,6},{8,9},{9,8},{10,11... | collective-permute-start | bytes 196616 | tf_op jit(solution)/shard_map/ppermute | solution.py:16
  4.5 6.1 %collective-permute-start = (bf16[8,4096]{1,0:T(8,128)(2,1)}, bf16[8,4096]{1,0:T(8,128)(2,1)S(1)}, u32[]{:S(2)}, u32[]{:S(2)}) collective-permute-start(bf16[8,4096]{1,0:T(8,128)(2,1)} %param.5), channel_id=1, source_target_pairs={{0,4},{1,5},{2,6},{3,7},{4,0},{5,1},{6,2},{7,3},{8,12},{9,13},{10,... | collective-permute-start | bytes 196616 | tf_op jit(solution)/shard_map/ppermute | solution.py:16
  7.1 11.8 %collective-permute-start.5 = (bf16[8,4096]{1,0:T(8,128)(2,1)}, bf16[8,4096]{1,0:T(8,128)(2,1)S(1)}, u32[]{:S(2)}, u32[]{:S(2)}) collective-permute-start(bf16[8,4096]{1,0:T(8,128)(2,1)} %param.5), channel_id=1, source_target_pairs={{0,3},{1,2},{2,1},{3,0},{4,7},{5,6},{6,5},{7,4},{8,11},{9,10},{10,... | collective-permute-start | bytes 196616 | tf_op jit(solution)/shard_map/ppermute | solution.py:16
  10.6 8.3 %collective-permute-start.6 = (bf16[8,4096]{1,0:T(8,128)(2,1)S(1)}, bf16[8,4096]{1,0:T(8,128)(2,1)S(1)}, u32[]{:S(2)}, u32[]{:S(2)}) collective-permute-start(bf16[8,4096]{1,0:T(8,128)(2,1)S(1)} %collective-permute-done.after), channel_id=1, source_target_pairs={{0,3},{1,2},{2,1},{3,0},{4,7},{5,6},{6,5},{7,4},{8,11},{9,10},{10,... | collective-permute-start | bytes 196616 | tf_op jit(solution)/shard_map/ppermute | solution.py:16
  10.9 7.9 %collective-permute-start.4 = (bf16[8,4096]{1,0:T(8,128)(2,1)S(1)}, bf16[8,4096]{1,0:T(8,128)(2,1)S(1)}, u32[]{:S(2)}, u32[]{:S(2)}) collective-permute-start(bf16[8,4096]{1,0:T(8,128)(2,1)S(1)} %collective-permute-done.after), channel_id=1, source_target_pairs={{0,2},{1,3},{2,0},{3,1},{4,6},{5,7},{6,4},{7,5},{8,10},{9,11},{10,... | collective-permute-start | bytes 196616 | tf_op jit(solution)/shard_map/ppermute | solution.py:16
  12.7 6.1 %collective-permute-start.2 = (bf16[8,4096]{1,0:T(8,128)(2,1)S(1)}, bf16[8,4096]{1,0:T(8,128)(2,1)S(1)}, u32[]{:S(2)}, u32[]{:S(2)}) collective-permute-start(bf16[8,4096]{1,0:T(8,128)(2,1)S(1)} %collective-permute-done.after), channel_id=1, source_target_pairs={{0,1},{1,0},{2,3},{3,2},{4,5},{5,4},{6,7},{7,6},{8,9},{9,8},{10,11... | collective-permute-start | bytes 196616 | tf_op jit(solution)/shard_map/ppermute | solution.py:16
  25.0 3.9 %collective-permute-start.7 = (f32[2,24,128]{2,1,0:T(8,128)S(1)}, f32[2,24,128]{2,1,0:T(8,128)S(1)}, u32[]{:S(2)}, u32[]{:S(2)}) collective-permute-start(f32[2,24,128]{2,1,0:T(8,128)S(1)} %get-tuple-element.18), channel_id=1, source_target_pairs={{0,1},{1,0},{2,3},{3,2},{4,5},{5,4},{6,7},{7,6},{8,9},{9,8},{10,11... | collective-permute-start | bytes 73736 | tf_op jit(solution)/shard_map/ppermute | solution.py:16
  25.7 3.8 %collective-permute-start.8 = (f32[2,24,128]{2,1,0:T(8,128)S(1)}, f32[2,24,128]{2,1,0:T(8,128)S(1)}, u32[]{:S(2)}, u32[]{:S(2)}) collective-permute-start(f32[2,24,128]{2,1,0:T(8,128)S(1)} %get-tuple-element.19), channel_id=1, source_target_pairs={{0,2},{1,3},{2,0},{3,1},{4,6},{5,7},{6,4},{7,5},{8,10},{9,11},{10,... | collective-permute-start | bytes 73736 | tf_op jit(solution)/shard_map/ppermute | solution.py:16
  26.0 4.7 %collective-permute-start.9 = (f32[2,24,128]{2,1,0:T(8,128)S(1)}, f32[2,24,128]{2,1,0:T(8,128)S(1)}, u32[]{:S(2)}, u32[]{:S(2)}) collective-permute-start(f32[2,24,128]{2,1,0:T(8,128)S(1)} %get-tuple-element.20), channel_id=1, source_target_pairs={{0,3},{1,2},{2,1},{3,0},{4,7},{5,6},{6,5},{7,4},{8,11},{9,10},{10,... | collective-permute-start | bytes 73736 | tf_op jit(solution)/shard_map/ppermute | solution.py:16
  30.7 5.1 %collective-permute-start.10 = (f32[4,24,128]{2,1,0:T(8,128)S(1)}, f32[4,24,128]{2,1,0:T(8,128)S(1)}, u32[]{:S(2)}, u32[]{:S(2)}) collective-permute-start(f32[4,24,128]{2,1,0:T(8,128)S(1)} %pad_maximum_fusion), channel_id=1, source_target_pairs={{0,4},{1,5},{2,6},{3,7},{4,0},{5,1},{6,2},{7,3},{8,12},{9,13},{10,... | collective-permute-start | bytes 147464 | tf_op jit(solution)/shard_map/ppermute | solution.py:16

commit v3 on v2

v3 whole, which is shorter than its diff:
```python
import functools

import jax
import jax.numpy as jnp
from jax import lax
from jax.experimental import pallas as pl
from jax.experimental.pallas import tpu as pltpu
from jax.sharding import PartitionSpec as P

BLK = 128
CAP = 16
NEAR = 4
ORDER = (0, 3, 1, 2)
FIRST = (0, 4)
SECOND = (0, 3, 1, 2)
PAD = 8


def exchange(x, n, mask):
    return lax.ppermute(x, "vocab", [(i, i ^ mask) for i in range(n)])


def split(n, rows_dev):
    beams = n * rows_dev
    at = lax.broadcasted_iota(jnp.int32, (beams, beams), 0)
    to = lax.broadcasted_iota(jnp.int32, (beams, beams), 1)
    shift = rows_dev.bit_length() - 1
    same = (at >> shift) == (to >> shift)
    return same.astype(jnp.bfloat16), (same & (at < to)).astype(jnp.bfloat16)


def mark_kernel(me_ref, out_ref):
    out_ref[...] = jnp.full(out_ref.shape, me_ref[0], jnp.int32)


def counts(a, b):
    return jnp.dot(a, b, preferred_element_type=jnp.float32)


def index_kernel(
    n,
    rows_dev,
    blocks_dev,
    me_ref,
    ids_hbm,
    valid_hbm,
    order_hbm,
    mark,
    after,
    hidden_hbm,
    src_ref,
    rows_ref,
    place_ref,
    own_ref,
    ids_ref,
    valid_ref,
    order_ref,
    sems,
):
    copies = [
        pltpu.make_async_copy(ids_hbm, ids_ref, sems.at[0]),
        pltpu.make_async_copy(valid_hbm, valid_ref, sems.at[1]),
        pltpu.make_async_copy(order_hbm, order_ref, sems.at[2]),
    ]
    own = pltpu.make_async_copy(hidden_hbm, own_ref, sems.at[3])
    for copy in copies + [own]:
        copy.start()
    for copy in copies:
        copy.wait()
    me = me_ref[0]
    slots, beams = ids_ref.shape
    shift = rows_dev.bit_length() - 1
    apart = (order_ref[...] >> shift) ^ me
    near = apart & (NEAR - 1)
    place = sum(jnp.where(near == mask, i, 0) for i, mask in enumerate(ORDER))
    row_of = ((place * (n // NEAR) + (apart >> (NEAR.bit_length() - 1)) + n - 1) & (n - 1)) * rows_dev
    row_of = row_of + (order_ref[...] & (rows_dev - 1))
    rows_ref[...] = jnp.full(rows_ref.shape, -1, jnp.int32)
    rows_ref[:, : order_ref.shape[1]] = row_of

    ids = ids_ref[...]
    same, earlier = split(n, rows_dev)
    k_at = lax.broadcasted_iota(jnp.int32, (slots, slots), 0)
    k_to = lax.broadcasted_iota(jnp.int32, (slots, slots), 1)
    below = (k_to < k_at).astype(jnp.bfloat16)

    def rank(on):
        ones = jnp.where(on, 1.0, 0.0).astype(jnp.bfloat16)
        return (counts(ones, earlier) + counts(below, counts(ones, same).astype(jnp.bfloat16))).astype(jnp.int32)

    at = jnp.zeros((slots, beams), jnp.int32)
    for d in range(n):
        on = (ids >= d * blocks_dev) & (ids < (d + 1) * blocks_dev)
        at = jnp.where(on, (me ^ d) * CAP + rank(on), at)
    k_index = lax.broadcasted_iota(jnp.int32, (slots, beams), 0)
    at = jnp.where(k_index < valid_ref[...], at, -1)
    row_index = lax.broadcasted_iota(jnp.int32, (slots, beams), 1)
    total = place_ref.shape[1]
    for r in range(rows_dev):
        column = jnp.sum(jnp.where(row_index == me * rows_dev + r, at, 0), axis=1, keepdims=True)
        hit = lax.broadcasted_iota(jnp.int32, (slots, total), 1) == column
        place_ref[r * slots : (r + 1) * slots, :] = jnp.where(hit, 1.0, 0.0)
    first = me * blocks_dev
    mine = (ids >= first) & (ids < first + blocks_dev)
    my_rank = jnp.where(mine, rank(mine), -1)
    local = ids - first
    owner = (
        (lax.broadcasted_iota(jnp.int32, (beams, n), 0) >> shift) == lax.broadcasted_iota(jnp.int32, (beams, n), 1)
    ).astype(jnp.bfloat16)
    rows = jnp.broadcast_to(row_of, (slots, beams))

    def gathered(value):
        picked = [jnp.sum(jnp.where(my_rank == j, value, 0), axis=0, keepdims=True) for j in range(CAP)]
        table = jnp.concatenate(picked, axis=0).astype(jnp.float32).astype(jnp.bfloat16)
        return counts(table, owner).astype(jnp.int32)

    src_ref[...] = gathered(local) * beams + gathered(rows)
    own.wait()


def second_masks(n):
    used = functools.reduce(lambda a, b: a | b, FIRST)
    masks = [mask for mask in range(n) if mask & used == 0]
    return [mask for mask in SECOND if mask in masks] + [mask for mask in masks if mask not in SECOND]


def score_kernel(n, me_ref, src_vmem, rows_ref, x_ref, head_ref, *refs):
    outs, (logits, src_ref, sem) = refs[: len(FIRST)], refs[len(FIRST) :]
    copy = pltpu.make_async_copy(src_vmem, src_ref, sem)
    copy.start()
    beams = x_ref.shape[0]
    blocks = head_ref.shape[1] // BLK
    group = 8 if blocks % 8 == 0 else 1
    for j in range(0, blocks, group):
        product = jnp.dot(x_ref[...], head_ref[:, j * BLK : (j + group) * BLK], preferred_element_type=jnp.float32)
        for i in range(group):
            logits[(j + i) * beams : (j + i + 1) * beams, :] = product[:, i * BLK : (i + 1) * BLK]
    most = functools.reduce(jnp.maximum, [logits[j * beams : (j + 1) * beams, :] for j in range(blocks)])
    most = jnp.max(most, axis=1, keepdims=True)
    total = sum(jnp.exp(logits[j * beams : (j + 1) * beams, :] - most) for j in range(blocks))
    lse = most + jnp.log(jnp.sum(total, axis=1, keepdims=True))
    hit = lax.broadcasted_iota(jnp.int32, (beams, rows_ref.shape[1]), 0) == rows_ref[...]
    ordered = jnp.sum(jnp.where(hit, lse, jnp.float32(0.0)), axis=0, keepdims=True)
    ordered = jnp.broadcast_to(ordered, (PAD, rows_ref.shape[1]))
    copy.wait()
    me = me_ref[0]
    second = second_masks(n)
    for i, a in enumerate(FIRST):
        for j, b in enumerate(second):
            owner = me ^ (a ^ b)
            for k in range(CAP):
                outs[i][j * CAP + k : j * CAP + k + 1, :] = logits[pl.ds(src_ref[k, owner], 1), :]
        for c in range(rows_ref.shape[1] // BLK):
            first = len(second) * CAP + c * PAD
            outs[i][first : first + PAD, :] = ordered[:, c * BLK : (c + 1) * BLK]


def place_kernel(n, rows_dev, slots, me_ref, place_ref, *refs):
    second = second_masks(n)
    own, others = refs[: len(FIRST)], refs[len(FIRST) : len(FIRST) + len(second) - 1]
    out_ref, held, stats = refs[-3:]
    wide = stats.shape[1] // BLK
    for i, a in enumerate(FIRST):
        for j, b in enumerate(second):
            d = a ^ b
            if j == 0:
                tiles, lse = own[i][:CAP, :], [own[i][len(second) * CAP + c * PAD : len(second) * CAP + c * PAD + 1, :] for c in range(wide)]
            else:
                tiles = others[j - 1][i * CAP : (i + 1) * CAP, :]
                lse = [others[j - 1][len(FIRST) * CAP + c * PAD + i : len(FIRST) * CAP + c * PAD + i + 1, :] for c in range(wide)]
            held[d * CAP : (d + 1) * CAP, :] = tiles
            for c in range(wide):
                stats[d : d + 1, c * BLK : (c + 1) * BLK] = lse[c]
    most = jnp.max(stats[...], axis=0, keepdims=True)
    lse = most + jnp.log(jnp.sum(jnp.exp(stats[...] - most), axis=0, keepdims=True))
    lane = lax.broadcasted_iota(jnp.int32, (rows_dev, stats.shape[1]), 1)
    row = lax.broadcasted_iota(jnp.int32, (rows_dev, stats.shape[1]), 0)
    lse = jnp.sum(jnp.where(lane == me_ref[0] * rows_dev + row, lse, jnp.float32(0.0)), axis=1, keepdims=True)
    left = held[...]
    place = place_ref[...].astype(jnp.bfloat16)
    tiles = jnp.zeros((rows_dev * slots, BLK), jnp.float32)
    for _ in range(3):
        part = left.astype(jnp.bfloat16)
        tiles += jnp.dot(place, part, preferred_element_type=jnp.float32)
        left -= part.astype(jnp.float32)
    valid = jnp.sum(place_ref[...], axis=1, keepdims=True) > 0
    for r in range(rows_dev):
        at = slice(r * slots, (r + 1) * slots)
        out_ref[r] = jnp.where(valid[at], tiles[at] - lse[r : r + 1, :], jnp.float32(0.0))


def in_vmem(x):
    return pltpu.with_memory_space_constraint(x, pltpu.VMEM)


def in_hbm(x):
    return pltpu.with_memory_space_constraint(x, pltpu.HBM)


def body(n, hidden, head, block_ids, valid_count, beam_order):
    me = lax.axis_index("vocab").astype(jnp.int32).reshape(1)
    rows_dev = hidden.shape[0]
    beams, slots = block_ids.shape
    blocks_dev = head.shape[1] // BLK
    fars = n // NEAR
    width = -(-beams // BLK) * BLK
    second = second_masks(n)
    anywhere = pl.BlockSpec(memory_space=pl.ANY)
    vmem = pl.BlockSpec(memory_space=pltpu.VMEM)
    smem = pl.BlockSpec(memory_space=pltpu.SMEM)
    hbm = pl.BlockSpec(memory_space=pltpu.HBM)

    far = [exchange(hidden, n, NEAR * f) for f in range(1, fars)]
    near = [exchange(hidden, n, mask) for mask in ORDER[1:]]
    far = far[0] if fars == 2 else jnp.concatenate(far, axis=0)
    mark = pl.pallas_call(
        mark_kernel,
        out_shape=jax.ShapeDtypeStruct((8, BLK), jnp.int32),
        in_specs=[smem],
        out_specs=vmem,
        cost_estimate=pl.CostEstimate(flops=2 * 10**10, bytes_accessed=0, transcendentals=0),
        compiler_params=pltpu.CompilerParams(vmem_limit_bytes=2**20),
        name="mark",
    )(me)

    src, row_of, place, kept = pl.pallas_call(
        functools.partial(index_kernel, n, rows_dev, blocks_dev),
        out_shape=[
            jax.ShapeDtypeStruct((CAP, n), jnp.int32),
            jax.ShapeDtypeStruct((1, width), jnp.int32),
            jax.ShapeDtypeStruct((rows_dev * slots, n * CAP), jnp.float32),
            pltpu.VMEM(hidden.shape, hidden.dtype),
        ],
        in_specs=[smem, hbm, hbm, hbm, anywhere, anywhere, hbm],
        out_specs=[vmem] * 4,
        scratch_shapes=[
            pltpu.VMEM((slots, beams), jnp.int32),
            pltpu.VMEM((1, beams), jnp.int32),
            pltpu.VMEM((1, beams), jnp.int32),
            pltpu.SemaphoreType.DMA((4,)),
        ],
        compiler_params=pltpu.CompilerParams(vmem_limit_bytes=4 * 2**20),
        name="index",
    )(
        me,
        in_hbm(block_ids.T),
        in_hbm(valid_count.reshape(1, beams)),
        in_hbm(beam_order.reshape(1, beams)),
        mark,
        far,
        in_hbm(hidden),
    )

    passed = [exchange(far, n, mask) for mask in ORDER[1:]]
    x = jnp.concatenate([far] + [part for pair in zip(near, passed) for part in pair] + [kept], axis=0)

    extra = width // BLK * PAD
    sent = pl.pallas_call(
        functools.partial(score_kernel, n),
        out_shape=[jax.ShapeDtypeStruct((len(second) * CAP + extra, BLK), jnp.float32)] * len(FIRST),
        in_specs=[smem, vmem, vmem, vmem, vmem],
        out_specs=[vmem] * len(FIRST),
        scratch_shapes=[
            pltpu.VMEM((blocks_dev * beams, BLK), jnp.float32),
            pltpu.SMEM((CAP, n), jnp.int32),
            pltpu.SemaphoreType.DMA,
        ],
        compiler_params=pltpu.CompilerParams(vmem_limit_bytes=24 * 2**20),
        name="score",
    )(me, in_vmem(src), in_vmem(row_of), in_vmem(x), in_vmem(head))

    own = [sent[0]] + [exchange(part, n, mask) for part, mask in zip(sent[1:], FIRST[1:])]
    at = lax.broadcasted_iota(jnp.int32, (extra, BLK), 0) % PAD
    stats = functools.reduce(
        lambda whole, i: jnp.where(at == i, own[i][len(second) * CAP :], whole), range(1, len(FIRST)), own[0][len(second) * CAP :]
    )
    others = [
        exchange(jnp.concatenate([part[j * CAP : (j + 1) * CAP] for part in own] + [stats]), n, mask)
        for j, mask in enumerate(second)
        if j
    ]
    return pl.pallas_call(
        functools.partial(place_kernel, n, rows_dev, slots),
        out_shape=jax.ShapeDtypeStruct((rows_dev, slots, BLK), jnp.float32),
        in_specs=[smem] + [vmem] * (1 + len(FIRST) + len(others)),
        out_specs=vmem,
        scratch_shapes=[pltpu.VMEM((n * CAP, BLK), jnp.float32), pltpu.VMEM((n, width), jnp.float32)],
        name="place",
    )(me, in_vmem(place), *map(in_vmem, own), *map(in_vmem, others))


def solution(mesh):
    return jax.shard_map(
        functools.partial(body, mesh.shape["vocab"]),
        mesh=mesh,
        in_specs=(P(("grp", "vocab"), None), P(None, "vocab"), P("grp", None), P("grp"), P("grp")),
        out_specs=P(("grp", "vocab"), None, None),
        check_vma=False,
    )
```

time: 37.6 us -> 33.5 us (0.89)
  Pallas kernels: 12.3 us -> 8.1 us
    pallas_call x2 -> x3, Pallas kernels: 10.7 us -> 7.3 us  [the longest x1 4.94 us: body(): pl.pallas_call(functools.partial(score_kernel, n), out_shape=[jax.ShapeDt...]
    pallas_call x1, Pallas kernels: 1.61 us -> 0.8 us  [body(): pl.pallas_call(functools.partial(place_kernel, n, rows_dev, slots), out_s...]
    unnamed x7 -> x9, local copies, waits for them, and re-layouts: 0.92 us -> 0.86 us
  transfers between devices with their start and end apart: 11 -> 11, of which waited for: 5 -> 6; matrix products, arithmetic and copies ran while one was open for 2% -> 0% of each run, Pallas kernels for 12% -> 7%
where the time goes in v3:
time: 33.5 us; the launch traced here: 33.4 us
  starting transfers between devices  17.2 us (51%)
  Pallas kernels  8.1 us (24%)
  waiting for transfers between devices  7 us (21%)
  local copies, waits for them, and re-layouts  0.87 us (3%)
    ppermute x11, starting transfers between devices, exchange(): return lax.ppermute(x, 'vocab', [(i, i ^ mask) for i in range(n)])  17.2 us
    ppermute x11, waiting for transfers between devices, exchange(): return lax.ppermute(x, 'vocab', [(i, i ^ mask) for i in range(n)])  7 us
    pallas_call x1, Pallas kernels, body(): pl.pallas_call(functools.partial(score_kernel, n), out_shape=[jax.ShapeDt...  4.94 us
    pallas_call x1, Pallas kernels, body(): pl.pallas_call(functools.partial(index_kernel, n, rows_dev, blocks_dev),...  2.35 us
    unnamed x9, local copies, waits for them, and re-layouts  0.86 us
    pallas_call x1, Pallas kernels, body(): pl.pallas_call(functools.partial(place_kernel, n, rows_dev, slots), out_s...  0.8 us
  transfers between devices with their start and end apart: 11, of which 6 were waited for; matrix products, arithmetic and copies ran while one was open for 0% of the time, Pallas kernels for 7%

profile of v3, /device:TPU:0, one launch (start us, length us, event | category | flops | bytes accessed | tf_op | source)
XLA Modules:
  0.0 33.4 jit_solution(7187799256741579351)
XLA Ops:
  0.0 4.0 %collective-permute-start = (bf16[8,4096]{1,0:T(8,128)(2,1)}, bf16[8,4096]{1,0:T(8,128)(2,1)S(1)}, u32[]{:S(2)}, u32[]{:S(2)}) collective-permute-start(bf16[8,4096]{1,0:T(8,128)(2,1)} %hidden_hbm.1), channel_id=1, source_target_pairs={{0,4},{1,5},{2,6},{3,7},{4,0},{5,1},{6,2},{7,3},{8,12},{9,13},{10,... | collective-permute-start | bytes 196616 | tf_op jit(solution)/shard_map/ppermute | solution.py:20
  4.0 2.5 %collective-permute-start.1 = (bf16[8,4096]{1,0:T(8,128)(2,1)}, bf16[8,4096]{1,0:T(8,128)(2,1)S(1)}, u32[]{:S(2)}, u32[]{:S(2)}) collective-permute-start(bf16[8,4096]{1,0:T(8,128)(2,1)} %hidden_hbm.1), channel_id=1, source_target_pairs={{0,3},{1,2},{2,1},{3,0},{4,7},{5,6},{6,5},{7,4},{8,11},{9,10},{10,... | collective-permute-start | bytes 196616 | tf_op jit(solution)/shard_map/ppermute | solution.py:20
  6.6 0.5 %collective-permute-start.3 = (bf16[8,4096]{1,0:T(8,128)(2,1)}, bf16[8,4096]{1,0:T(8,128)(2,1)S(1)}, u32[]{:S(2)}, u32[]{:S(2)}) collective-permute-start(bf16[8,4096]{1,0:T(8,128)(2,1)} %hidden_hbm.1), channel_id=1, source_target_pairs={{0,1},{1,0},{2,3},{3,2},{4,5},{5,4},{6,7},{7,6},{8,9},{9,8},{10,11... | collective-permute-start | bytes 196616 | tf_op jit(solution)/shard_map/ppermute | solution.py:20
  7.1 0.4 %collective-permute-start.5 = (bf16[8,4096]{1,0:T(8,128)(2,1)}, bf16[8,4096]{1,0:T(8,128)(2,1)S(1)}, u32[]{:S(2)}, u32[]{:S(2)}) collective-permute-start(bf16[8,4096]{1,0:T(8,128)(2,1)} %hidden_hbm.1), channel_id=1, source_target_pairs={{0,2},{1,3},{2,0},{3,1},{4,6},{5,7},{6,4},{7,5},{8,10},{9,11},{10,... | collective-permute-start | bytes 196616 | tf_op jit(solution)/shard_map/ppermute | solution.py:20
  7.5 0.0 copy-start
  7.5 0.0 collective-permute-done.after
  7.6 2.6 %collective-permute-start.2 = (bf16[8,4096]{1,0:T(8,128)(2,1)S(1)}, bf16[8,4096]{1,0:T(8,128)(2,1)S(1)}, u32[]{:S(2)}, u32[]{:S(2)}) collective-permute-start(bf16[8,4096]{1,0:T(8,128)(2,1)S(1)} %collective-permute-done.after), channel_id=1, source_target_pairs={{0,3},{1,2},{2,1},{3,0},{4,7},{5,6},{6,5},{7,4},{8,11},{9,10},{10,... | collective-permute-start | bytes 196616 | tf_op jit(solution)/shard_map/ppermute | solution.py:20
  10.2 0.5 %collective-permute-start.4 = (bf16[8,4096]{1,0:T(8,128)(2,1)S(1)}, bf16[8,4096]{1,0:T(8,128)(2,1)S(1)}, u32[]{:S(2)}, u32[]{:S(2)}) collective-permute-start(bf16[8,4096]{1,0:T(8,128)(2,1)S(1)} %collective-permute-done.after), channel_id=1, source_target_pairs={{0,1},{1,0},{2,3},{3,2},{4,5},{5,4},{6,7},{7,6},{8,9},{9,8},{10,11... | collective-permute-start | bytes 196616 | tf_op jit(solution)/shard_map/ppermute | solution.py:20
  10.7 0.0 collective-permute-done.1
  10.7 1.0 %collective-permute-start.6 = (bf16[8,4096]{1,0:T(8,128)(2,1)S(1)}, bf16[8,4096]{1,0:T(8,128)(2,1)S(1)}, u32[]{:S(2)}, u32[]{:S(2)}) collective-permute-start(bf16[8,4096]{1,0:T(8,128)(2,1)S(1)} %collective-permute-done.after), channel_id=1, source_target_pairs={{0,2},{1,3},{2,0},{3,1},{4,6},{5,7},{6,4},{7,5},{8,10},{9,11},{10,... | collective-permute-start | bytes 196616 | tf_op jit(solution)/shard_map/ppermute | solution.py:20
  11.7 2.4 %index.1 = (s32[16,8]{1,0:T(8,128)S(1)}, s32[1,128]{1,0:T(1,128)S(1)}, f32[128,128]{1,0:T(8,128)S(1)}, bf16[8,4096]{1,0:T(8,128)(2,1)S(1)}) custom-call(s32[1]{0:T(128)} %bitcast.me_ref, s32[16,64]{1,0:T(8,128)} %bitcast.4, s32[1,64]{1,0:T(1,128)} %bitcast.5, s32[1,64]{1,0:T(1,128)} %bitcast.6, s32[8,128]{1,0:T(8,128)S(1)} %mark.1, ...), custom_call_target="tpu_custom_call" | custom-call | tf_op jit(solution)/shard_map/index/pallas_call | solution.py:226
  14.1 0.0 collective-permute-done.2
  14.1 0.0 collective-permute-done.3
  14.1 0.5 %collective-permute-done.4 = bf16[8,4096]{1,0:T(8,128)(2,1)S(1)} collective-permute-done((bf16[8,4096]{1,0:T(8,128)(2,1)S(1)}, bf16[8,4096]{1,0:T(8,128)(2,1)S(1)}, u32[]{:S(2)}, u32[]{:S(2)}) %collective-permute-start.4) | collective-permute-done | bytes 65568 | tf_op jit(solution)/shard_map/ppermute | solution.py:20
  14.6 0.0 collective-permute-done.5
  14.6 0.3 collective-permute-done.6
  15.0 0.8 %copy-done = bf16[4096,3072]{1,0:T(8,128)(2,1)S(1)} copy-done((bf16[4096,3072]{1,0:T(8,128)(2,1)S(1)}, bf16[4096,3072]{1,0:T(8,128)(2,1)}, u32[]{:S(2)}) %copy-start) | copy-done | bytes 25165848
  15.8 4.9 %score.1 = (f32[72,128]{1,0:T(8,128)S(1)}, f32[72,128]{1,0:T(8,128)S(1)}) custom-call(s32[1]{0:T(128)} %bitcast.me_ref, s32[16,8]{1,0:T(8,128)S(1)} %get-tuple-element.12.src_vmem, s32[1,128]{1,0:T(1,128)S(1)} %get-tuple-element.13.rows_ref, bf16[64,4096]{1,0:T(8,128)(2,1)S(1)} %constant_dynamic-update-slice_fusion.x_ref, bf16[4096,3072]{1,0:T(8,128)(2,1)S(1)} %copy-done), custom_call_target="tpu_custom_call" | custom-call | tf_op jit(solution)/shard_map/score/pallas_call | solution.py:258
  20.7 2.0 %collective-permute-start.7 = (f32[72,128]{1,0:T(8,128)S(1)}, f32[72,128]{1,0:T(8,128)S(1)}, u32[]{:S(2)}, u32[]{:S(2)}) collective-permute-start(f32[72,128]{1,0:T(8,128)S(1)} %get-tuple-element.16), channel_id=1, source_target_pairs={{0,4},{1,5},{2,6},{3,7},{4,0},{5,1},{6,2},{7,3},{8,12},{9,13},{10,... | collective-permute-start | bytes 110600 | tf_op jit(solution)/shard_map/ppermute | solution.py:20
  22.7 2.9 %collective-permute-done.7.refs_1_ = f32[72,128]{1,0:T(8,128)S(1)} collective-permute-done((f32[72,128]{1,0:T(8,128)S(1)}, f32[72,128]{1,0:T(8,128)S(1)}, u32[]{:S(2)}, u32[]{:S(2)}) %collective-permute-start.7) | collective-permute-done | bytes 36896 | tf_op jit(solution)/shard_map/ppermute | solution.py:20
  25.6 0.1 slice_select_fusion
  25.7 1.6 %collective-permute-start.10 = (f32[40,128]{1,0:T(8,128)S(1)}, f32[40,128]{1,0:T(8,128)S(1)}, u32[]{:S(2)}, u32[]{:S(2)}) collective-permute-start(f32[40,128]{1,0:T(8,128)S(1)} %get-tuple-element.23), channel_id=1, source_target_pairs={{0,2},{1,3},{2,0},{3,1},{4,6},{5,7},{6,4},{7,5},{8,10},{9,11},{10,... | collective-permute-start | bytes 61448 | tf_op jit(solution)/shard_map/ppermute | solution.py:20
  27.4 1.4 %collective-permute-start.8 = (f32[40,128]{1,0:T(8,128)S(1)}, f32[40,128]{1,0:T(8,128)S(1)}, u32[]{:S(2)}, u32[]{:S(2)}) collective-permute-start(f32[40,128]{1,0:T(8,128)S(1)} %get-tuple-element.25), channel_id=1, source_target_pairs={{0,3},{1,2},{2,1},{3,0},{4,7},{5,6},{6,5},{7,4},{8,11},{9,10},{10,... | collective-permute-start | bytes 61448 | tf_op jit(solution)/shard_map/ppermute | solution.py:20
  28.8 0.5 %collective-permute-start.9 = (f32[40,128]{1,0:T(8,128)S(1)}, f32[40,128]{1,0:T(8,128)S(1)}, u32[]{:S(2)}, u32[]{:S(2)}) collective-permute-start(f32[40,128]{1,0:T(8,128)S(1)} %get-tuple-element.24), channel_id=1, source_target_pairs={{0,1},{1,0},{2,3},{3,2},{4,5},{5,4},{6,7},{7,6},{8,9},{9,8},{10,11... | collective-permute-start | bytes 61448 | tf_op jit(solution)/shard_map/ppermute | solution.py:20
  29.3 0.3 collective-permute-done.10.refs_4_
  29.6 2.5 %collective-permute-done.8.refs_2_ = f32[40,128]{1,0:T(8,128)S(1)} collective-permute-done((f32[40,128]{1,0:T(8,128)S(1)}, f32[40,128]{1,0:T(8,128)S(1)}, u32[]{:S(2)}, u32[]{:S(2)}) %collective-permute-start.8) | collective-permute-done | bytes 20512 | tf_op jit(solution)/shard_map/ppermute | solution.py:20
  32.1 0.5 %collective-permute-done.9.refs_3_ = f32[40,128]{1,0:T(8,128)S(1)} collective-permute-done((f32[40,128]{1,0:T(8,128)S(1)}, f32[40,128]{1,0:T(8,128)S(1)}, u32[]{:S(2)}, u32[]{:S(2)}) %collective-permute-start.9) | collective-permute-done | bytes 20512 | tf_op jit(solution)/shard_map/ppermute | solution.py:20
  32.6 0.8 %place.1 = f32[8,16,128]{2,1,0:T(8,128)} custom-call(s32[1]{0:T(128)} %bitcast.me_ref, f32[128,128]{1,0:T(8,128)S(1)} %get-tuple-element.11.place_ref, f32[72,128]{1,0:T(8,128)S(1)} %get-tuple-element.15.refs_0_, f32[72,128]{1,0:T(8,128)S(1)} %collective-permute-done.7.refs_1_, f32[40,128]{1,0:T(8,128)S(1)} %collective-permute-done.8.refs_2_, ...), custom_call_target="tpu_custom_call" | custom-call | tf_op jit(solution)/shard_map/place/pallas_call | solution.py:282
  (14 shorter events, 0.1 us)
Async XLA Ops:
  0.0 7.5 %collective-permute-start = (bf16[8,4096]{1,0:T(8,128)(2,1)}, bf16[8,4096]{1,0:T(8,128)(2,1)S(1)}, u32[]{:S(2)}, u32[]{:S(2)}) collective-permute-start(bf16[8,4096]{1,0:T(8,128)(2,1)} %hidden_hbm.1), channel_id=1, source_target_pairs={{0,4},{1,5},{2,6},{3,7},{4,0},{5,1},{6,2},{7,3},{8,12},{9,13},{10,... | collective-permute-start | bytes 196616 | tf_op jit(solution)/shard_map/ppermute | solution.py:20
  4.0 6.6 %collective-permute-start.1 = (bf16[8,4096]{1,0:T(8,128)(2,1)}, bf16[8,4096]{1,0:T(8,128)(2,1)S(1)}, u32[]{:S(2)}, u32[]{:S(2)}) collective-permute-start(bf16[8,4096]{1,0:T(8,128)(2,1)} %hidden_hbm.1), channel_id=1, source_target_pairs={{0,3},{1,2},{2,1},{3,0},{4,7},{5,6},{6,5},{7,4},{8,11},{9,10},{10,... | collective-permute-start | bytes 196616 | tf_op jit(solution)/shard_map/ppermute | solution.py:20
  6.6 7.5 %collective-permute-start.3 = (bf16[8,4096]{1,0:T(8,128)(2,1)}, bf16[8,4096]{1,0:T(8,128)(2,1)S(1)}, u32[]{:S(2)}, u32[]{:S(2)}) collective-permute-start(bf16[8,4096]{1,0:T(8,128)(2,1)} %hidden_hbm.1), channel_id=1, source_target_pairs={{0,1},{1,0},{2,3},{3,2},{4,5},{5,4},{6,7},{7,6},{8,9},{9,8},{10,11... | collective-permute-start | bytes 196616 | tf_op jit(solution)/shard_map/ppermute | solution.py:20
  7.1 7.5 %collective-permute-start.5 = (bf16[8,4096]{1,0:T(8,128)(2,1)}, bf16[8,4096]{1,0:T(8,128)(2,1)S(1)}, u32[]{:S(2)}, u32[]{:S(2)}) collective-permute-start(bf16[8,4096]{1,0:T(8,128)(2,1)} %hidden_hbm.1), channel_id=1, source_target_pairs={{0,2},{1,3},{2,0},{3,1},{4,6},{5,7},{6,4},{7,5},{8,10},{9,11},{10,... | collective-permute-start | bytes 196616 | tf_op jit(solution)/shard_map/ppermute | solution.py:20
  7.5 8.2 %copy-start = (bf16[4096,3072]{1,0:T(8,128)(2,1)S(1)}, bf16[4096,3072]{1,0:T(8,128)(2,1)}, u32[]{:S(2)}) copy-start(bf16[4096,3072]{1,0:T(8,128)(2,1)} %head_ref.1) | copy-start | bytes 75497472
  7.6 6.5 %collective-permute-start.2 = (bf16[8,4096]{1,0:T(8,128)(2,1)S(1)}, bf16[8,4096]{1,0:T(8,128)(2,1)S(1)}, u32[]{:S(2)}, u32[]{:S(2)}) collective-permute-start(bf16[8,4096]{1,0:T(8,128)(2,1)S(1)} %collective-permute-done.after), channel_id=1, source_target_pairs={{0,3},{1,2},{2,1},{3,0},{4,7},{5,6},{6,5},{7,4},{8,11},{9,10},{10,... | collective-permute-start | bytes 196616 | tf_op jit(solution)/shard_map/ppermute | solution.py:20
  10.2 4.5 %collective-permute-start.4 = (bf16[8,4096]{1,0:T(8,128)(2,1)S(1)}, bf16[8,4096]{1,0:T(8,128)(2,1)S(1)}, u32[]{:S(2)}, u32[]{:S(2)}) collective-permute-start(bf16[8,4096]{1,0:T(8,128)(2,1)S(1)} %collective-permute-done.after), channel_id=1, source_target_pairs={{0,1},{1,0},{2,3},{3,2},{4,5},{5,4},{6,7},{7,6},{8,9},{9,8},{10,11... | collective-permute-start | bytes 196616 | tf_op jit(solution)/shard_map/ppermute | solution.py:20
  10.7 4.3 %collective-permute-start.6 = (bf16[8,4096]{1,0:T(8,128)(2,1)S(1)}, bf16[8,4096]{1,0:T(8,128)(2,1)S(1)}, u32[]{:S(2)}, u32[]{:S(2)}) collective-permute-start(bf16[8,4096]{1,0:T(8,128)(2,1)S(1)} %collective-permute-done.after), channel_id=1, source_target_pairs={{0,2},{1,3},{2,0},{3,1},{4,6},{5,7},{6,4},{7,5},{8,10},{9,11},{10,... | collective-permute-start | bytes 196616 | tf_op jit(solution)/shard_map/ppermute | solution.py:20
  20.7 4.9 %collective-permute-start.7 = (f32[72,128]{1,0:T(8,128)S(1)}, f32[72,128]{1,0:T(8,128)S(1)}, u32[]{:S(2)}, u32[]{:S(2)}) collective-permute-start(f32[72,128]{1,0:T(8,128)S(1)} %get-tuple-element.16), channel_id=1, source_target_pairs={{0,4},{1,5},{2,6},{3,7},{4,0},{5,1},{6,2},{7,3},{8,12},{9,13},{10,... | collective-permute-start | bytes 110600 | tf_op jit(solution)/shard_map/ppermute | solution.py:20
  25.7 3.8 %collective-permute-start.10 = (f32[40,128]{1,0:T(8,128)S(1)}, f32[40,128]{1,0:T(8,128)S(1)}, u32[]{:S(2)}, u32[]{:S(2)}) collective-permute-start(f32[40,128]{1,0:T(8,128)S(1)} %get-tuple-element.23), channel_id=1, source_target_pairs={{0,2},{1,3},{2,0},{3,1},{4,6},{5,7},{6,4},{7,5},{8,10},{9,11},{10,... | collective-permute-start | bytes 61448 | tf_op jit(solution)/shard_map/ppermute | solution.py:20
  27.4 4.7 %collective-permute-start.8 = (f32[40,128]{1,0:T(8,128)S(1)}, f32[40,128]{1,0:T(8,128)S(1)}, u32[]{:S(2)}, u32[]{:S(2)}) collective-permute-start(f32[40,128]{1,0:T(8,128)S(1)} %get-tuple-element.25), channel_id=1, source_target_pairs={{0,3},{1,2},{2,1},{3,0},{4,7},{5,6},{6,5},{7,4},{8,11},{9,10},{10,... | collective-permute-start | bytes 61448 | tf_op jit(solution)/shard_map/ppermute | solution.py:20
  28.8 3.8 %collective-permute-start.9 = (f32[40,128]{1,0:T(8,128)S(1)}, f32[40,128]{1,0:T(8,128)S(1)}, u32[]{:S(2)}, u32[]{:S(2)}) collective-permute-start(f32[40,128]{1,0:T(8,128)S(1)} %get-tuple-element.24), channel_id=1, source_target_pairs={{0,1},{1,0},{2,3},{3,2},{4,5},{5,4},{6,7},{7,6},{8,9},{9,8},{10,11... | collective-permute-start | bytes 61448 | tf_op jit(solution)/shard_map/ppermute | solution.py:20

commit v4 on v3

--- a/solution.py
+++ b/solution.py
@@ -10,9 +10,12 @@
 BLK = 128
 CAP = 16
 NEAR = 4
-ORDER = (0, 3, 1, 2)
+OWN = (3, 1, 2)
+PASSED = (1, 3, 2)
 FIRST = (0, 4)
 SECOND = (0, 3, 1, 2)
+GROUP = 2
+ROWS = 128
 PAD = 8
 
 
@@ -72,8 +75,13 @@
     shift = rows_dev.bit_length() - 1
     apart = (order_ref[...] >> shift) ^ me
     near = apart & (NEAR - 1)
-    place = sum(jnp.where(near == mask, i, 0) for i, mask in enumerate(ORDER))
-    row_of = ((place * (n // NEAR) + (apart >> (NEAR.bit_length() - 1)) + n - 1) & (n - 1)) * rows_dev
+    far = apart >> (NEAR.bit_length() - 1)
+    fars = n // NEAR - 1
+    row_of = jnp.where(far == 0, n - 1, far - 1)
+    for i in range(NEAR - 1):
+        row_of = jnp.where((near == OWN[i]) & (far == 0), fars + i, row_of)
+        row_of = jnp.where((near == PASSED[i]) & (far > 0), fars * (i + 1) + NEAR - 2 + far, row_of)
+    row_of = row_of * rows_dev
     row_of = row_of + (order_ref[...] & (rows_dev - 1))
     rows_ref[...] = jnp.full(rows_ref.shape, -1, jnp.int32)
     rows_ref[:, : order_ref.shape[1]] = row_of
@@ -130,15 +138,20 @@
     copy.start()
     beams = x_ref.shape[0]
     blocks = head_ref.shape[1] // BLK
-    group = 8 if blocks % 8 == 0 else 1
+    group = GROUP if blocks % GROUP == 0 else 1
+    wide = x_ref[...] if beams >= ROWS else jnp.concatenate([x_ref[...]] * (ROWS // beams))
+    most = total = None
     for j in range(0, blocks, group):
-        product = jnp.dot(x_ref[...], head_ref[:, j * BLK : (j + group) * BLK], preferred_element_type=jnp.float32)
-        for i in range(group):
-            logits[(j + i) * beams : (j + i + 1) * beams, :] = product[:, i * BLK : (i + 1) * BLK]
-    most = functools.reduce(jnp.maximum, [logits[j * beams : (j + 1) * beams, :] for j in range(blocks)])
-    most = jnp.max(most, axis=1, keepdims=True)
-    total = sum(jnp.exp(logits[j * beams : (j + 1) * beams, :] - most) for j in range(blocks))
-    lse = most + jnp.log(jnp.sum(total, axis=1, keepdims=True))
+        product = jnp.dot(wide, head_ref[:, j * BLK : (j + group) * BLK], preferred_element_type=jnp.float32)[:beams]
+        tiles = [product[:, i * BLK : (i + 1) * BLK] for i in range(group)]
+        for i, tile in enumerate(tiles):
+            logits[(j + i) * beams : (j + i + 1) * beams, :] = tile
+        higher = functools.reduce(jnp.maximum, tiles if most is None else [most] + tiles)
+        terms = [jnp.exp(tile - higher) for tile in tiles]
+        total = sum(terms if total is None else [total * jnp.exp(most - higher)] + terms)
+        most = higher
+    peak = jnp.max(most, axis=1, keepdims=True)
+    lse = peak + jnp.log(jnp.sum(total * jnp.exp(most - peak), axis=1, keepdims=True))
     hit = lax.broadcasted_iota(jnp.int32, (beams, rows_ref.shape[1]), 0) == rows_ref[...]
     ordered = jnp.sum(jnp.where(hit, lse, jnp.float32(0.0)), axis=0, keepdims=True)
     ordered = jnp.broadcast_to(ordered, (PAD, rows_ref.shape[1]))
@@ -211,7 +224,7 @@
     hbm = pl.BlockSpec(memory_space=pltpu.HBM)
 
     far = [exchange(hidden, n, NEAR * f) for f in range(1, fars)]
-    near = [exchange(hidden, n, mask) for mask in ORDER[1:]]
+    near = [exchange(hidden, n, mask) for mask in OWN]
     far = far[0] if fars == 2 else jnp.concatenate(far, axis=0)
     mark = pl.pallas_call(
         mark_kernel,
@@ -251,8 +264,8 @@
         in_hbm(hidden),
     )
 
-    passed = [exchange(far, n, mask) for mask in ORDER[1:]]
-    x = jnp.concatenate([far] + [part for pair in zip(near, passed) for part in pair] + [kept], axis=0)
+    passed = [exchange(far, n, mask) for mask in PASSED]
+    x = jnp.concatenate([far] + near + passed + [kept], axis=0)
 
     extra = width // BLK * PAD
     sent = pl.pallas_call(

time: 33.5 us -> 32.4 us (0.967)
  Pallas kernels: 8.1 us -> 6.98 us
    pallas_call x1, Pallas kernels: 4.94 us -> 3.82 us  [body(): pl.pallas_call(functools.partial(score_kernel, n), out_shape=[jax.ShapeDt...]
where the time goes in v4:
time: 32.4 us; the launch traced here: 32.2 us
  starting transfers between devices  17.2 us (53%)
  waiting for transfers between devices  7 us (22%)
  Pallas kernels  6.98 us (22%)
  local copies, waits for them, and re-layouts  0.87 us (3%)
    ppermute x11, starting transfers between devices, exchange(): return lax.ppermute(x, 'vocab', [(i, i ^ mask) for i in range(n)])  17.2 us
    ppermute x11, waiting for transfers between devices, exchange(): return lax.ppermute(x, 'vocab', [(i, i ^ mask) for i in range(n)])  7 us
    pallas_call x1, Pallas kernels, body(): pl.pallas_call(functools.partial(score_kernel, n), out_shape=[jax.ShapeDt...  3.82 us
    pallas_call x1, Pallas kernels, body(): pl.pallas_call(functools.partial(index_kernel, n, rows_dev, blocks_dev),...  2.36 us
    unnamed x9, local copies, waits for them, and re-layouts  0.86 us
    pallas_call x1, Pallas kernels, body(): pl.pallas_call(functools.partial(place_kernel, n, rows_dev, slots), out_s...  0.8 us
  transfers between devices with their start and end apart: 11, of which 6 were waited for; matrix products, arithmetic and copies ran while one was open for 0% of the time, Pallas kernels for 7%

profile of v4, /device:TPU:0, one launch (start us, length us, event | category | flops | bytes accessed | tf_op | source)
XLA Modules:
  0.0 32.2 jit_solution(18191433682264862287)
XLA Ops:
  0.0 4.0 %collective-permute-start = (bf16[8,4096]{1,0:T(8,128)(2,1)}, bf16[8,4096]{1,0:T(8,128)(2,1)S(1)}, u32[]{:S(2)}, u32[]{:S(2)}) collective-permute-start(bf16[8,4096]{1,0:T(8,128)(2,1)} %hidden_hbm.1), channel_id=1, source_target_pairs={{0,4},{1,5},{2,6},{3,7},{4,0},{5,1},{6,2},{7,3},{8,12},{9,13},{10,... | collective-permute-start | bytes 196616 | tf_op jit(solution)/shard_map/ppermute | solution.py:23
  4.0 2.5 %collective-permute-start.1 = (bf16[8,4096]{1,0:T(8,128)(2,1)}, bf16[8,4096]{1,0:T(8,128)(2,1)S(1)}, u32[]{:S(2)}, u32[]{:S(2)}) collective-permute-start(bf16[8,4096]{1,0:T(8,128)(2,1)} %hidden_hbm.1), channel_id=1, source_target_pairs={{0,3},{1,2},{2,1},{3,0},{4,7},{5,6},{6,5},{7,4},{8,11},{9,10},{10,... | collective-permute-start | bytes 196616 | tf_op jit(solution)/shard_map/ppermute | solution.py:23
  6.6 0.5 %collective-permute-start.2 = (bf16[8,4096]{1,0:T(8,128)(2,1)}, bf16[8,4096]{1,0:T(8,128)(2,1)S(1)}, u32[]{:S(2)}, u32[]{:S(2)}) collective-permute-start(bf16[8,4096]{1,0:T(8,128)(2,1)} %hidden_hbm.1), channel_id=1, source_target_pairs={{0,1},{1,0},{2,3},{3,2},{4,5},{5,4},{6,7},{7,6},{8,9},{9,8},{10,11... | collective-permute-start | bytes 196616 | tf_op jit(solution)/shard_map/ppermute | solution.py:23
  7.1 0.4 %collective-permute-start.3 = (bf16[8,4096]{1,0:T(8,128)(2,1)}, bf16[8,4096]{1,0:T(8,128)(2,1)S(1)}, u32[]{:S(2)}, u32[]{:S(2)}) collective-permute-start(bf16[8,4096]{1,0:T(8,128)(2,1)} %hidden_hbm.1), channel_id=1, source_target_pairs={{0,2},{1,3},{2,0},{3,1},{4,6},{5,7},{6,4},{7,5},{8,10},{9,11},{10,... | collective-permute-start | bytes 196616 | tf_op jit(solution)/shard_map/ppermute | solution.py:23
  7.5 0.0 copy-start
  7.5 0.0 collective-permute-done.after
  7.6 1.6 %collective-permute-start.4 = (bf16[8,4096]{1,0:T(8,128)(2,1)S(1)}, bf16[8,4096]{1,0:T(8,128)(2,1)S(1)}, u32[]{:S(2)}, u32[]{:S(2)}) collective-permute-start(bf16[8,4096]{1,0:T(8,128)(2,1)S(1)} %collective-permute-done.after), channel_id=1, source_target_pairs={{0,1},{1,0},{2,3},{3,2},{4,5},{5,4},{6,7},{7,6},{8,9},{9,8},{10,11... | collective-permute-start | bytes 196616 | tf_op jit(solution)/shard_map/ppermute | solution.py:23
  9.2 1.5 %collective-permute-start.5 = (bf16[8,4096]{1,0:T(8,128)(2,1)S(1)}, bf16[8,4096]{1,0:T(8,128)(2,1)S(1)}, u32[]{:S(2)}, u32[]{:S(2)}) collective-permute-start(bf16[8,4096]{1,0:T(8,128)(2,1)S(1)} %collective-permute-done.after), channel_id=1, source_target_pairs={{0,3},{1,2},{2,1},{3,0},{4,7},{5,6},{6,5},{7,4},{8,11},{9,10},{10,... | collective-permute-start | bytes 196616 | tf_op jit(solution)/shard_map/ppermute | solution.py:23
  10.7 0.0 collective-permute-done.1
  10.7 1.0 %collective-permute-start.6 = (bf16[8,4096]{1,0:T(8,128)(2,1)S(1)}, bf16[8,4096]{1,0:T(8,128)(2,1)S(1)}, u32[]{:S(2)}, u32[]{:S(2)}) collective-permute-start(bf16[8,4096]{1,0:T(8,128)(2,1)S(1)} %collective-permute-done.after), channel_id=1, source_target_pairs={{0,2},{1,3},{2,0},{3,1},{4,6},{5,7},{6,4},{7,5},{8,10},{9,11},{10,... | collective-permute-start | bytes 196616 | tf_op jit(solution)/shard_map/ppermute | solution.py:23
  11.7 0.5 %collective-permute-done.2 = bf16[8,4096]{1,0:T(8,128)(2,1)S(1)} collective-permute-done((bf16[8,4096]{1,0:T(8,128)(2,1)}, bf16[8,4096]{1,0:T(8,128)(2,1)S(1)}, u32[]{:S(2)}, u32[]{:S(2)}) %collective-permute-start.2) | collective-permute-done | bytes 65568 | tf_op jit(solution)/shard_map/ppermute | solution.py:23
  12.2 0.0 collective-permute-done.3
  12.2 2.4 %index.1 = (s32[16,8]{1,0:T(8,128)S(1)}, s32[1,128]{1,0:T(1,128)S(1)}, f32[128,128]{1,0:T(8,128)S(1)}, bf16[8,4096]{1,0:T(8,128)(2,1)S(1)}) custom-call(s32[1]{0:T(128)} %bitcast.me_ref, s32[16,64]{1,0:T(8,128)} %bitcast.4, s32[1,64]{1,0:T(1,128)} %bitcast.5, s32[1,64]{1,0:T(1,128)} %bitcast.6, s32[8,128]{1,0:T(8,128)S(1)} %mark.1, ...), custom_call_target="tpu_custom_call" | custom-call | tf_op jit(solution)/shard_map/index/pallas_call | solution.py:239
  14.6 0.0 collective-permute-done.4
  14.6 0.0 collective-permute-done.5
  14.6 0.3 collective-permute-done.6
  15.0 0.8 %copy-done = bf16[4096,3072]{1,0:T(8,128)(2,1)S(1)} copy-done((bf16[4096,3072]{1,0:T(8,128)(2,1)S(1)}, bf16[4096,3072]{1,0:T(8,128)(2,1)}, u32[]{:S(2)}) %copy-start) | copy-done | bytes 25165848
  15.8 3.8 %score.1 = (f32[72,128]{1,0:T(8,128)S(1)}, f32[72,128]{1,0:T(8,128)S(1)}) custom-call(s32[1]{0:T(128)} %bitcast.me_ref, s32[16,8]{1,0:T(8,128)S(1)} %get-tuple-element.12.src_vmem, s32[1,128]{1,0:T(1,128)S(1)} %get-tuple-element.13.rows_ref, bf16[64,4096]{1,0:T(8,128)(2,1)S(1)} %constant_dynamic-update-slice_fusion.x_ref, bf16[4096,3072]{1,0:T(8,128)(2,1)S(1)} %copy-done), custom_call_target="tpu_custom_call" | custom-call | tf_op jit(solution)/shard_map/score/pallas_call | solution.py:271
  19.6 2.0 %collective-permute-start.7 = (f32[72,128]{1,0:T(8,128)S(1)}, f32[72,128]{1,0:T(8,128)S(1)}, u32[]{:S(2)}, u32[]{:S(2)}) collective-permute-start(f32[72,128]{1,0:T(8,128)S(1)} %get-tuple-element.16), channel_id=1, source_target_pairs={{0,4},{1,5},{2,6},{3,7},{4,0},{5,1},{6,2},{7,3},{8,12},{9,13},{10,... | collective-permute-start | bytes 110600 | tf_op jit(solution)/shard_map/ppermute | solution.py:23
  21.6 2.9 %collective-permute-done.7.refs_1_ = f32[72,128]{1,0:T(8,128)S(1)} collective-permute-done((f32[72,128]{1,0:T(8,128)S(1)}, f32[72,128]{1,0:T(8,128)S(1)}, u32[]{:S(2)}, u32[]{:S(2)}) %collective-permute-start.7) | collective-permute-done | bytes 36896 | tf_op jit(solution)/shard_map/ppermute | solution.py:23
  24.5 0.1 slice_select_fusion
  24.6 1.6 %collective-permute-start.10 = (f32[40,128]{1,0:T(8,128)S(1)}, f32[40,128]{1,0:T(8,128)S(1)}, u32[]{:S(2)}, u32[]{:S(2)}) collective-permute-start(f32[40,128]{1,0:T(8,128)S(1)} %get-tuple-element.23), channel_id=1, source_target_pairs={{0,2},{1,3},{2,0},{3,1},{4,6},{5,7},{6,4},{7,5},{8,10},{9,11},{10,... | collective-permute-start | bytes 61448 | tf_op jit(solution)/shard_map/ppermute | solution.py:23
  26.2 1.4 %collective-permute-start.8 = (f32[40,128]{1,0:T(8,128)S(1)}, f32[40,128]{1,0:T(8,128)S(1)}, u32[]{:S(2)}, u32[]{:S(2)}) collective-permute-start(f32[40,128]{1,0:T(8,128)S(1)} %get-tuple-element.25), channel_id=1, source_target_pairs={{0,3},{1,2},{2,1},{3,0},{4,7},{5,6},{6,5},{7,4},{8,11},{9,10},{10,... | collective-permute-start | bytes 61448 | tf_op jit(solution)/shard_map/ppermute | solution.py:23
  27.6 0.5 %collective-permute-start.9 = (f32[40,128]{1,0:T(8,128)S(1)}, f32[40,128]{1,0:T(8,128)S(1)}, u32[]{:S(2)}, u32[]{:S(2)}) collective-permute-start(f32[40,128]{1,0:T(8,128)S(1)} %get-tuple-element.24), channel_id=1, source_target_pairs={{0,1},{1,0},{2,3},{3,2},{4,5},{5,4},{6,7},{7,6},{8,9},{9,8},{10,11... | collective-permute-start | bytes 61448 | tf_op jit(solution)/shard_map/ppermute | solution.py:23
  28.2 0.3 collective-permute-done.10.refs_4_
  28.5 2.5 %collective-permute-done.8.refs_2_ = f32[40,128]{1,0:T(8,128)S(1)} collective-permute-done((f32[40,128]{1,0:T(8,128)S(1)}, f32[40,128]{1,0:T(8,128)S(1)}, u32[]{:S(2)}, u32[]{:S(2)}) %collective-permute-start.8) | collective-permute-done | bytes 20512 | tf_op jit(solution)/shard_map/ppermute | solution.py:23
  30.9 0.5 %collective-permute-done.9.refs_3_ = f32[40,128]{1,0:T(8,128)S(1)} collective-permute-done((f32[40,128]{1,0:T(8,128)S(1)}, f32[40,128]{1,0:T(8,128)S(1)}, u32[]{:S(2)}, u32[]{:S(2)}) %collective-permute-start.9) | collective-permute-done | bytes 20512 | tf_op jit(solution)/shard_map/ppermute | solution.py:23
  31.4 0.8 %place.1 = f32[8,16,128]{2,1,0:T(8,128)} custom-call(s32[1]{0:T(128)} %bitcast.me_ref, f32[128,128]{1,0:T(8,128)S(1)} %get-tuple-element.11.place_ref, f32[72,128]{1,0:T(8,128)S(1)} %get-tuple-element.15.refs_0_, f32[72,128]{1,0:T(8,128)S(1)} %collective-permute-done.7.refs_1_, f32[40,128]{1,0:T(8,128)S(1)} %collective-permute-done.8.refs_2_, ...), custom_call_target="tpu_custom_call" | custom-call | tf_op jit(solution)/shard_map/place/pallas_call | solution.py:295
  (14 shorter events, 0.1 us)
Async XLA Ops:
  0.0 7.5 %collective-permute-start = (bf16[8,4096]{1,0:T(8,128)(2,1)}, bf16[8,4096]{1,0:T(8,128)(2,1)S(1)}, u32[]{:S(2)}, u32[]{:S(2)}) collective-permute-start(bf16[8,4096]{1,0:T(8,128)(2,1)} %hidden_hbm.1), channel_id=1, source_target_pairs={{0,4},{1,5},{2,6},{3,7},{4,0},{5,1},{6,2},{7,3},{8,12},{9,13},{10,... | collective-permute-start | bytes 196616 | tf_op jit(solution)/shard_map/ppermute | solution.py:23
  4.0 6.6 %collective-permute-start.1 = (bf16[8,4096]{1,0:T(8,128)(2,1)}, bf16[8,4096]{1,0:T(8,128)(2,1)S(1)}, u32[]{:S(2)}, u32[]{:S(2)}) collective-permute-start(bf16[8,4096]{1,0:T(8,128)(2,1)} %hidden_hbm.1), channel_id=1, source_target_pairs={{0,3},{1,2},{2,1},{3,0},{4,7},{5,6},{6,5},{7,4},{8,11},{9,10},{10,... | collective-permute-start | bytes 196616 | tf_op jit(solution)/shard_map/ppermute | solution.py:23
  6.6 5.6 %collective-permute-start.2 = (bf16[8,4096]{1,0:T(8,128)(2,1)}, bf16[8,4096]{1,0:T(8,128)(2,1)S(1)}, u32[]{:S(2)}, u32[]{:S(2)}) collective-permute-start(bf16[8,4096]{1,0:T(8,128)(2,1)} %hidden_hbm.1), channel_id=1, source_target_pairs={{0,1},{1,0},{2,3},{3,2},{4,5},{5,4},{6,7},{7,6},{8,9},{9,8},{10,11... | collective-permute-start | bytes 196616 | tf_op jit(solution)/shard_map/ppermute | solution.py:23
  7.1 5.1 %collective-permute-start.3 = (bf16[8,4096]{1,0:T(8,128)(2,1)}, bf16[8,4096]{1,0:T(8,128)(2,1)S(1)}, u32[]{:S(2)}, u32[]{:S(2)}) collective-permute-start(bf16[8,4096]{1,0:T(8,128)(2,1)} %hidden_hbm.1), channel_id=1, source_target_pairs={{0,2},{1,3},{2,0},{3,1},{4,6},{5,7},{6,4},{7,5},{8,10},{9,11},{10,... | collective-permute-start | bytes 196616 | tf_op jit(solution)/shard_map/ppermute | solution.py:23
  7.5 8.2 %copy-start = (bf16[4096,3072]{1,0:T(8,128)(2,1)S(1)}, bf16[4096,3072]{1,0:T(8,128)(2,1)}, u32[]{:S(2)}) copy-start(bf16[4096,3072]{1,0:T(8,128)(2,1)} %head_ref.1) | copy-start | bytes 75497472
  7.6 7.0 %collective-permute-start.4 = (bf16[8,4096]{1,0:T(8,128)(2,1)S(1)}, bf16[8,4096]{1,0:T(8,128)(2,1)S(1)}, u32[]{:S(2)}, u32[]{:S(2)}) collective-permute-start(bf16[8,4096]{1,0:T(8,128)(2,1)S(1)} %collective-permute-done.after), channel_id=1, source_target_pairs={{0,1},{1,0},{2,3},{3,2},{4,5},{5,4},{6,7},{7,6},{8,9},{9,8},{10,11... | collective-permute-start | bytes 196616 | tf_op jit(solution)/shard_map/ppermute | solution.py:23
  9.2 5.4 %collective-permute-start.5 = (bf16[8,4096]{1,0:T(8,128)(2,1)S(1)}, bf16[8,4096]{1,0:T(8,128)(2,1)S(1)}, u32[]{:S(2)}, u32[]{:S(2)}) collective-permute-start(bf16[8,4096]{1,0:T(8,128)(2,1)S(1)} %collective-permute-done.after), channel_id=1, source_target_pairs={{0,3},{1,2},{2,1},{3,0},{4,7},{5,6},{6,5},{7,4},{8,11},{9,10},{10,... | collective-permute-start | bytes 196616 | tf_op jit(solution)/shard_map/ppermute | solution.py:23
  10.7 4.3 %collective-permute-start.6 = (bf16[8,4096]{1,0:T(8,128)(2,1)S(1)}, bf16[8,4096]{1,0:T(8,128)(2,1)S(1)}, u32[]{:S(2)}, u32[]{:S(2)}) collective-permute-start(bf16[8,4096]{1,0:T(8,128)(2,1)S(1)} %collective-permute-done.after), channel_id=1, source_target_pairs={{0,2},{1,3},{2,0},{3,1},{4,6},{5,7},{6,4},{7,5},{8,10},{9,11},{10,... | collective-permute-start | bytes 196616 | tf_op jit(solution)/shard_map/ppermute | solution.py:23
  19.6 4.9 %collective-permute-start.7 = (f32[72,128]{1,0:T(8,128)S(1)}, f32[72,128]{1,0:T(8,128)S(1)}, u32[]{:S(2)}, u32[]{:S(2)}) collective-permute-start(f32[72,128]{1,0:T(8,128)S(1)} %get-tuple-element.16), channel_id=1, source_target_pairs={{0,4},{1,5},{2,6},{3,7},{4,0},{5,1},{6,2},{7,3},{8,12},{9,13},{10,... | collective-permute-start | bytes 110600 | tf_op jit(solution)/shard_map/ppermute | solution.py:23
  24.6 3.8 %collective-permute-start.10 = (f32[40,128]{1,0:T(8,128)S(1)}, f32[40,128]{1,0:T(8,128)S(1)}, u32[]{:S(2)}, u32[]{:S(2)}) collective-permute-start(f32[40,128]{1,0:T(8,128)S(1)} %get-tuple-element.23), channel_id=1, source_target_pairs={{0,2},{1,3},{2,0},{3,1},{4,6},{5,7},{6,4},{7,5},{8,10},{9,11},{10,... | collective-permute-start | bytes 61448 | tf_op jit(solution)/shard_map/ppermute | solution.py:23
  26.2 4.7 %collective-permute-start.8 = (f32[40,128]{1,0:T(8,128)S(1)}, f32[40,128]{1,0:T(8,128)S(1)}, u32[]{:S(2)}, u32[]{:S(2)}) collective-permute-start(f32[40,128]{1,0:T(8,128)S(1)} %get-tuple-element.25), channel_id=1, source_target_pairs={{0,3},{1,2},{2,1},{3,0},{4,7},{5,6},{6,5},{7,4},{8,11},{9,10},{10,... | collective-permute-start | bytes 61448 | tf_op jit(solution)/shard_map/ppermute | solution.py:23
  27.6 3.8 %collective-permute-start.9 = (f32[40,128]{1,0:T(8,128)S(1)}, f32[40,128]{1,0:T(8,128)S(1)}, u32[]{:S(2)}, u32[]{:S(2)}) collective-permute-start(f32[40,128]{1,0:T(8,128)S(1)} %get-tuple-element.24), channel_id=1, source_target_pairs={{0,1},{1,0},{2,3},{3,2},{4,5},{5,4},{6,7},{7,6},{8,9},{9,8},{10,11... | collective-permute-start | bytes 61448 | tf_op jit(solution)/shard_map/ppermute | solution.py:23

commit v5 on v4

--- a/solution.py
+++ b/solution.py
@@ -10,10 +10,10 @@
 BLK = 128
 CAP = 16
 NEAR = 4
-OWN = (3, 1, 2)
-PASSED = (1, 3, 2)
+EARLY = (2, 1)
+LATE = (3, 2, 1)
 FIRST = (0, 4)
-SECOND = (0, 3, 1, 2)
+SECOND = (0, 3, 2, 1)
 GROUP = 2
 ROWS = 128
 PAD = 8
@@ -38,6 +38,14 @@
 
 def counts(a, b):
     return jnp.dot(a, b, preferred_element_type=jnp.float32)
+
+
+def layout(n):
+    far = list(range(NEAR, n, NEAR))
+    masks = list(EARLY)
+    for near in LATE:
+        masks += [near ^ mask for mask in ([] if near in EARLY else [0]) + far]
+    return masks + [0] + far
 
 
 def index_kernel(
@@ -50,11 +58,9 @@
     order_hbm,
     mark,
     after,
-    hidden_hbm,
     src_ref,
     rows_ref,
     place_ref,
-    own_ref,
     ids_ref,
     valid_ref,
     order_ref,
@@ -65,8 +71,7 @@
         pltpu.make_async_copy(valid_hbm, valid_ref, sems.at[1]),
         pltpu.make_async_copy(order_hbm, order_ref, sems.at[2]),
     ]
-    own = pltpu.make_async_copy(hidden_hbm, own_ref, sems.at[3])
-    for copy in copies + [own]:
+    for copy in copies:
         copy.start()
     for copy in copies:
         copy.wait()
@@ -74,14 +79,7 @@
     slots, beams = ids_ref.shape
     shift = rows_dev.bit_length() - 1
     apart = (order_ref[...] >> shift) ^ me
-    near = apart & (NEAR - 1)
-    far = apart >> (NEAR.bit_length() - 1)
-    fars = n // NEAR - 1
-    row_of = jnp.where(far == 0, n - 1, far - 1)
-    for i in range(NEAR - 1):
-        row_of = jnp.where((near == OWN[i]) & (far == 0), fars + i, row_of)
-        row_of = jnp.where((near == PASSED[i]) & (far > 0), fars * (i + 1) + NEAR - 2 + far, row_of)
-    row_of = row_of * rows_dev
+    row_of = sum(jnp.where(apart == mask, i * rows_dev, 0) for i, mask in enumerate(layout(n)))
     row_of = row_of + (order_ref[...] & (rows_dev - 1))
     rows_ref[...] = jnp.full(rows_ref.shape, -1, jnp.int32)
     rows_ref[:, : order_ref.shape[1]] = row_of
@@ -123,7 +121,6 @@
         return counts(table, owner).astype(jnp.int32)
 
     src_ref[...] = gathered(local) * beams + gathered(rows)
-    own.wait()
 
 
 def second_masks(n):
@@ -224,7 +221,7 @@
     hbm = pl.BlockSpec(memory_space=pltpu.HBM)
 
     far = [exchange(hidden, n, NEAR * f) for f in range(1, fars)]
-    near = [exchange(hidden, n, mask) for mask in OWN]
+    near = [exchange(hidden, n, mask) for mask in EARLY]
     far = far[0] if fars == 2 else jnp.concatenate(far, axis=0)
     mark = pl.pallas_call(
         mark_kernel,
@@ -236,21 +233,20 @@
         name="mark",
     )(me)
 
-    src, row_of, place, kept = pl.pallas_call(
+    src, row_of, place = pl.pallas_call(
         functools.partial(index_kernel, n, rows_dev, blocks_dev),
         out_shape=[
             jax.ShapeDtypeStruct((CAP, n), jnp.int32),
             jax.ShapeDtypeStruct((1, width), jnp.int32),
             jax.ShapeDtypeStruct((rows_dev * slots, n * CAP), jnp.float32),
-            pltpu.VMEM(hidden.shape, hidden.dtype),
         ],
-        in_specs=[smem, hbm, hbm, hbm, anywhere, anywhere, hbm],
-        out_specs=[vmem] * 4,
+        in_specs=[smem, hbm, hbm, hbm, anywhere, anywhere],
+        out_specs=[vmem] * 3,
         scratch_shapes=[
             pltpu.VMEM((slots, beams), jnp.int32),
             pltpu.VMEM((1, beams), jnp.int32),
             pltpu.VMEM((1, beams), jnp.int32),
-            pltpu.SemaphoreType.DMA((4,)),
+            pltpu.SemaphoreType.DMA((3,)),
         ],
         compiler_params=pltpu.CompilerParams(vmem_limit_bytes=4 * 2**20),
         name="index",
@@ -261,11 +257,11 @@
         in_hbm(beam_order.reshape(1, beams)),
         mark,
         far,
-        in_hbm(hidden),
     )
 
-    passed = [exchange(far, n, mask) for mask in PASSED]
-    x = jnp.concatenate([far] + near + passed + [kept], axis=0)
+    both = jnp.concatenate([hidden, far], axis=0)
+    late = [exchange(far if mask in EARLY else both, n, mask) for mask in LATE]
+    x = jnp.concatenate([*near, *late, both], axis=0)
 
     extra = width // BLK * PAD
     sent = pl.pallas_call(

time: 32.4 us -> 31 us (0.957)
  waiting for transfers between devices: 7 us -> 6.03 us
  starting transfers between devices: 17.2 us -> 16.6 us
    ppermute x11 -> x10, waiting for transfers between devices: 7 us -> 6.03 us  [exchange(): return lax.ppermute(x, 'vocab', [(i, i ^ mask) for i in range(n)])]
    ppermute x11 -> x10, starting transfers between devices: 17.2 us -> 16.6 us  [exchange(): return lax.ppermute(x, 'vocab', [(i, i ^ mask) for i in range(n)])]
    unnamed x9 -> x10, local copies, waits for them, and re-layouts: 0.86 us -> 1.11 us
  transfers between devices with their start and end apart: 11 -> 10, of which waited for: 6 -> 7; matrix products, arithmetic and copies ran while one was open for 0% -> 0% of each run, Pallas kernels for 7% -> 8%
where the time goes in v5:
time: 31 us; the launch traced here: 30.9 us
  starting transfers between devices  16.6 us (54%)
  Pallas kernels  6.97 us (22%)
  waiting for transfers between devices  6.03 us (19%)
  local copies, waits for them, and re-layouts  1.12 us (4%)
    ppermute x10, starting transfers between devices, exchange(): return lax.ppermute(x, 'vocab', [(i, i ^ mask) for i in range(n)])  16.6 us
    ppermute x10, waiting for transfers between devices, exchange(): return lax.ppermute(x, 'vocab', [(i, i ^ mask) for i in range(n)])  6.03 us
    pallas_call x1, Pallas kernels, body(): pl.pallas_call(functools.partial(score_kernel, n), out_shape=[jax.ShapeDt...  3.81 us
    pallas_call x1, Pallas kernels, body(): pl.pallas_call(functools.partial(index_kernel, n, rows_dev, blocks_dev),...  2.35 us
    unnamed x10, local copies, waits for them, and re-layouts  1.11 us
    pallas_call x1, Pallas kernels, body(): pl.pallas_call(functools.partial(place_kernel, n, rows_dev, slots), out_s...  0.8 us
  transfers between devices with their start and end apart: 10, of which 7 were waited for; matrix products, arithmetic and copies ran while one was open for 0% of the time, Pallas kernels for 8%

profile of v5, /device:TPU:0, one launch (start us, length us, event | category | flops | bytes accessed | tf_op | source)
XLA Modules:
  0.0 30.9 jit_solution(12183291736907876616)
XLA Ops:
  0.0 4.0 %collective-permute-start = (bf16[8,4096]{1,0:T(8,128)(2,1)}, bf16[8,4096]{1,0:T(8,128)(2,1)S(1)}, u32[]{:S(2)}, u32[]{:S(2)}) collective-permute-start(bf16[8,4096]{1,0:T(8,128)(2,1)} %param.5), channel_id=1, source_target_pairs={{0,4},{1,5},{2,6},{3,7},{4,0},{5,1},{6,2},{7,3},{8,12},{9,13},{10,... | collective-permute-start | bytes 196616 | tf_op jit(solution)/shard_map/ppermute | solution.py:23
  4.0 1.6 %collective-permute-start.1 = (bf16[8,4096]{1,0:T(8,128)(2,1)}, bf16[8,4096]{1,0:T(8,128)(2,1)S(1)}, u32[]{:S(2)}, u32[]{:S(2)}) collective-permute-start(bf16[8,4096]{1,0:T(8,128)(2,1)} %param.5), channel_id=1, source_target_pairs={{0,2},{1,3},{2,0},{3,1},{4,6},{5,7},{6,4},{7,5},{8,10},{9,11},{10,... | collective-permute-start | bytes 196616 | tf_op jit(solution)/shard_map/ppermute | solution.py:23
  5.6 1.5 %collective-permute-start.2 = (bf16[8,4096]{1,0:T(8,128)(2,1)}, bf16[8,4096]{1,0:T(8,128)(2,1)S(1)}, u32[]{:S(2)}, u32[]{:S(2)}) collective-permute-start(bf16[8,4096]{1,0:T(8,128)(2,1)} %param.5), channel_id=1, source_target_pairs={{0,1},{1,0},{2,3},{3,2},{4,5},{5,4},{6,7},{7,6},{8,9},{9,8},{10,11... | collective-permute-start | bytes 196616 | tf_op jit(solution)/shard_map/ppermute | solution.py:23
  7.1 0.0 copy-start.1
  7.1 0.0 copy-start
  7.2 0.1 collective-permute-done.after
  7.3 0.7 %copy-done.1 = bf16[8,4096]{1,0:T(8,128)(2,1)S(1)} copy-done((bf16[8,4096]{1,0:T(8,128)(2,1)S(1)}, bf16[8,4096]{1,0:T(8,128)(2,1)}, u32[]{:S(2)}) %copy-start.1) | copy-done | bytes 65560
  8.0 1.7 %collective-permute-start.3 = (bf16[16,4096]{1,0:T(8,128)(2,1)S(1)}, bf16[16,4096]{1,0:T(8,128)(2,1)S(1)}, u32[]{:S(2)}, u32[]{:S(2)}) collective-permute-start(bf16[16,4096]{1,0:T(8,128)(2,1)S(1)} %pad_maximum_fusion), channel_id=1, source_target_pairs={{0,3},{1,2},{2,1},{3,0},{4,7},{5,6},{6,5},{7,4},{8,11},{9,10},{10,... | collective-permute-start | bytes 393224 | tf_op jit(solution)/shard_map/ppermute | solution.py:23
  9.7 1.0 %collective-permute-start.4 = (bf16[8,4096]{1,0:T(8,128)(2,1)S(1)}, bf16[8,4096]{1,0:T(8,128)(2,1)S(1)}, u32[]{:S(2)}, u32[]{:S(2)}) collective-permute-start(bf16[8,4096]{1,0:T(8,128)(2,1)S(1)} %collective-permute-done.after), channel_id=1, source_target_pairs={{0,2},{1,3},{2,0},{3,1},{4,6},{5,7},{6,4},{7,5},{8,10},{9,11},{10,... | collective-permute-start | bytes 196616 | tf_op jit(solution)/shard_map/ppermute | solution.py:23
  10.7 0.9 %collective-permute-start.5 = (bf16[8,4096]{1,0:T(8,128)(2,1)S(1)}, bf16[8,4096]{1,0:T(8,128)(2,1)S(1)}, u32[]{:S(2)}, u32[]{:S(2)}) collective-permute-start(bf16[8,4096]{1,0:T(8,128)(2,1)S(1)} %collective-permute-done.after), channel_id=1, source_target_pairs={{0,1},{1,0},{2,3},{3,2},{4,5},{5,4},{6,7},{7,6},{8,9},{9,8},{10,11... | collective-permute-start | bytes 196616 | tf_op jit(solution)/shard_map/ppermute | solution.py:23
  11.6 0.0 collective-permute-done.1
  11.6 0.0 collective-permute-done.2
  11.6 2.3 %index.1 = (s32[16,8]{1,0:T(8,128)S(1)}, s32[1,128]{1,0:T(1,128)S(1)}, f32[128,128]{1,0:T(8,128)S(1)}) custom-call(s32[1]{0:T(128)} %bitcast.me_ref, s32[16,64]{1,0:T(8,128)} %bitcast.4, s32[1,64]{1,0:T(1,128)} %bitcast.5, s32[1,64]{1,0:T(1,128)} %bitcast.6, s32[8,128]{1,0:T(8,128)S(1)} %mark.1, bf16[8,4096]{1,0:T(8,128)(2,1)S(1)} %collective-permute-done.after), custom_call_target="tpu_custom_call" | custom-call | tf_op jit(solution)/shard_map/index/pallas_call | solution.py:236
  14.0 0.1 collective-permute-done.3
  14.1 0.3 collective-permute-done.4
  14.4 0.6 %collective-permute-done.5 = bf16[8,4096]{1,0:T(8,128)(2,1)S(1)} collective-permute-done((bf16[8,4096]{1,0:T(8,128)(2,1)S(1)}, bf16[8,4096]{1,0:T(8,128)(2,1)S(1)}, u32[]{:S(2)}, u32[]{:S(2)}) %collective-permute-start.5) | collective-permute-done | bytes 65568 | tf_op jit(solution)/shard_map/ppermute | solution.py:23
  15.0 0.4 %copy-done = bf16[4096,3072]{1,0:T(8,128)(2,1)S(1)} copy-done((bf16[4096,3072]{1,0:T(8,128)(2,1)S(1)}, bf16[4096,3072]{1,0:T(8,128)(2,1)}, u32[]{:S(2)}) %copy-start) | copy-done | bytes 25165848
  15.4 3.8 %score.1 = (f32[72,128]{1,0:T(8,128)S(1)}, f32[72,128]{1,0:T(8,128)S(1)}) custom-call(s32[1]{0:T(128)} %bitcast.me_ref, s32[16,8]{1,0:T(8,128)S(1)} %get-tuple-element.11.src_vmem, s32[1,128]{1,0:T(1,128)S(1)} %get-tuple-element.12.rows_ref, bf16[64,4096]{1,0:T(8,128)(2,1)S(1)} %constant_dynamic-update-slice_fusion.x_ref, bf16[4096,3072]{1,0:T(8,128)(2,1)S(1)} %copy-done), custom_call_target="tpu_custom_call" | custom-call | tf_op jit(solution)/shard_map/score/pallas_call | solution.py:267
  19.2 2.3 %collective-permute-start.6 = (f32[72,128]{1,0:T(8,128)S(1)}, f32[72,128]{1,0:T(8,128)S(1)}, u32[]{:S(2)}, u32[]{:S(2)}) collective-permute-start(f32[72,128]{1,0:T(8,128)S(1)} %get-tuple-element.14), channel_id=1, source_target_pairs={{0,4},{1,5},{2,6},{3,7},{4,0},{5,1},{6,2},{7,3},{8,12},{9,13},{10,... | collective-permute-start | bytes 110600 | tf_op jit(solution)/shard_map/ppermute | solution.py:23
  21.5 2.6 %collective-permute-done.6.refs_1_ = f32[72,128]{1,0:T(8,128)S(1)} collective-permute-done((f32[72,128]{1,0:T(8,128)S(1)}, f32[72,128]{1,0:T(8,128)S(1)}, u32[]{:S(2)}, u32[]{:S(2)}) %collective-permute-start.6) | collective-permute-done | bytes 36896 | tf_op jit(solution)/shard_map/ppermute | solution.py:23
  24.1 0.1 slice_select_fusion
  24.2 2.0 %collective-permute-start.7 = (f32[40,128]{1,0:T(8,128)S(1)}, f32[40,128]{1,0:T(8,128)S(1)}, u32[]{:S(2)}, u32[]{:S(2)}) collective-permute-start(f32[40,128]{1,0:T(8,128)S(1)} %get-tuple-element.23), channel_id=1, source_target_pairs={{0,3},{1,2},{2,1},{3,0},{4,7},{5,6},{6,5},{7,4},{8,11},{9,10},{10,... | collective-permute-start | bytes 61448 | tf_op jit(solution)/shard_map/ppermute | solution.py:23
  26.3 0.0 collective-permute-start.8
  26.3 1.5 %collective-permute-start.9 = (f32[40,128]{1,0:T(8,128)S(1)}, f32[40,128]{1,0:T(8,128)S(1)}, u32[]{:S(2)}, u32[]{:S(2)}) collective-permute-start(f32[40,128]{1,0:T(8,128)S(1)} %get-tuple-element.21), channel_id=1, source_target_pairs={{0,1},{1,0},{2,3},{3,2},{4,5},{5,4},{6,7},{7,6},{8,9},{9,8},{10,11... | collective-permute-start | bytes 61448 | tf_op jit(solution)/shard_map/ppermute | solution.py:23
  27.8 1.2 %collective-permute-done.7.refs_2_ = f32[40,128]{1,0:T(8,128)S(1)} collective-permute-done((f32[40,128]{1,0:T(8,128)S(1)}, f32[40,128]{1,0:T(8,128)S(1)}, u32[]{:S(2)}, u32[]{:S(2)}) %collective-permute-start.7) | collective-permute-done | bytes 20512 | tf_op jit(solution)/shard_map/ppermute | solution.py:23
  29.0 1.1 %collective-permute-done.8.refs_3_ = f32[40,128]{1,0:T(8,128)S(1)} collective-permute-done((f32[40,128]{1,0:T(8,128)S(1)}, f32[40,128]{1,0:T(8,128)S(1)}, u32[]{:S(2)}, u32[]{:S(2)}) %collective-permute-start.8) | collective-permute-done | bytes 20512 | tf_op jit(solution)/shard_map/ppermute | solution.py:23
  30.0 0.0 collective-permute-done.9.refs_4_
  30.1 0.8 %place.1 = f32[8,16,128]{2,1,0:T(8,128)} custom-call(s32[1]{0:T(128)} %bitcast.me_ref, f32[128,128]{1,0:T(8,128)S(1)} %get-tuple-element.10.place_ref, f32[72,128]{1,0:T(8,128)S(1)} %get-tuple-element.13.refs_0_, f32[72,128]{1,0:T(8,128)S(1)} %collective-permute-done.6.refs_1_, f32[40,128]{1,0:T(8,128)S(1)} %collective-permute-done.7.refs_2_, ...), custom_call_target="tpu_custom_call" | custom-call | tf_op jit(solution)/shard_map/place/pallas_call | solution.py:291
  (14 shorter events, 0.1 us)
Async XLA Ops:
  0.0 7.3 %collective-permute-start = (bf16[8,4096]{1,0:T(8,128)(2,1)}, bf16[8,4096]{1,0:T(8,128)(2,1)S(1)}, u32[]{:S(2)}, u32[]{:S(2)}) collective-permute-start(bf16[8,4096]{1,0:T(8,128)(2,1)} %param.5), channel_id=1, source_target_pairs={{0,4},{1,5},{2,6},{3,7},{4,0},{5,1},{6,2},{7,3},{8,12},{9,13},{10,... | collective-permute-start | bytes 196616 | tf_op jit(solution)/shard_map/ppermute | solution.py:23
  4.0 7.5 %collective-permute-start.1 = (bf16[8,4096]{1,0:T(8,128)(2,1)}, bf16[8,4096]{1,0:T(8,128)(2,1)S(1)}, u32[]{:S(2)}, u32[]{:S(2)}) collective-permute-start(bf16[8,4096]{1,0:T(8,128)(2,1)} %param.5), channel_id=1, source_target_pairs={{0,2},{1,3},{2,0},{3,1},{4,6},{5,7},{6,4},{7,5},{8,10},{9,11},{10,... | collective-permute-start | bytes 196616 | tf_op jit(solution)/shard_map/ppermute | solution.py:23
  5.6 6.0 %collective-permute-start.2 = (bf16[8,4096]{1,0:T(8,128)(2,1)}, bf16[8,4096]{1,0:T(8,128)(2,1)S(1)}, u32[]{:S(2)}, u32[]{:S(2)}) collective-permute-start(bf16[8,4096]{1,0:T(8,128)(2,1)} %param.5), channel_id=1, source_target_pairs={{0,1},{1,0},{2,3},{3,2},{4,5},{5,4},{6,7},{7,6},{8,9},{9,8},{10,11... | collective-permute-start | bytes 196616 | tf_op jit(solution)/shard_map/ppermute | solution.py:23
  7.1 0.9 %copy-start.1 = (bf16[8,4096]{1,0:T(8,128)(2,1)S(1)}, bf16[8,4096]{1,0:T(8,128)(2,1)}, u32[]{:S(2)}) copy-start(bf16[8,4096]{1,0:T(8,128)(2,1)} %param.5) | copy-start | bytes 196612
  7.1 8.2 %copy-start = (bf16[4096,3072]{1,0:T(8,128)(2,1)S(1)}, bf16[4096,3072]{1,0:T(8,128)(2,1)}, u32[]{:S(2)}) copy-start(bf16[4096,3072]{1,0:T(8,128)(2,1)} %head_ref.1) | copy-start | bytes 75497472
  8.0 6.1 %collective-permute-start.3 = (bf16[16,4096]{1,0:T(8,128)(2,1)S(1)}, bf16[16,4096]{1,0:T(8,128)(2,1)S(1)}, u32[]{:S(2)}, u32[]{:S(2)}) collective-permute-start(bf16[16,4096]{1,0:T(8,128)(2,1)S(1)} %pad_maximum_fusion), channel_id=1, source_target_pairs={{0,3},{1,2},{2,1},{3,0},{4,7},{5,6},{6,5},{7,4},{8,11},{9,10},{10,... | collective-permute-start | bytes 393224 | tf_op jit(solution)/shard_map/ppermute | solution.py:23
  9.7 4.7 %collective-permute-start.4 = (bf16[8,4096]{1,0:T(8,128)(2,1)S(1)}, bf16[8,4096]{1,0:T(8,128)(2,1)S(1)}, u32[]{:S(2)}, u32[]{:S(2)}) collective-permute-start(bf16[8,4096]{1,0:T(8,128)(2,1)S(1)} %collective-permute-done.after), channel_id=1, source_target_pairs={{0,2},{1,3},{2,0},{3,1},{4,6},{5,7},{6,4},{7,5},{8,10},{9,11},{10,... | collective-permute-start | bytes 196616 | tf_op jit(solution)/shard_map/ppermute | solution.py:23
  10.7 4.3 %collective-permute-start.5 = (bf16[8,4096]{1,0:T(8,128)(2,1)S(1)}, bf16[8,4096]{1,0:T(8,128)(2,1)S(1)}, u32[]{:S(2)}, u32[]{:S(2)}) collective-permute-start(bf16[8,4096]{1,0:T(8,128)(2,1)S(1)} %collective-permute-done.after), channel_id=1, source_target_pairs={{0,1},{1,0},{2,3},{3,2},{4,5},{5,4},{6,7},{7,6},{8,9},{9,8},{10,11... | collective-permute-start | bytes 196616 | tf_op jit(solution)/shard_map/ppermute | solution.py:23
  19.2 4.9 %collective-permute-start.6 = (f32[72,128]{1,0:T(8,128)S(1)}, f32[72,128]{1,0:T(8,128)S(1)}, u32[]{:S(2)}, u32[]{:S(2)}) collective-permute-start(f32[72,128]{1,0:T(8,128)S(1)} %get-tuple-element.14), channel_id=1, source_target_pairs={{0,4},{1,5},{2,6},{3,7},{4,0},{5,1},{6,2},{7,3},{8,12},{9,13},{10,... | collective-permute-start | bytes 110600 | tf_op jit(solution)/shard_map/ppermute | solution.py:23
  24.2 4.7 %collective-permute-start.7 = (f32[40,128]{1,0:T(8,128)S(1)}, f32[40,128]{1,0:T(8,128)S(1)}, u32[]{:S(2)}, u32[]{:S(2)}) collective-permute-start(f32[40,128]{1,0:T(8,128)S(1)} %get-tuple-element.23), channel_id=1, source_target_pairs={{0,3},{1,2},{2,1},{3,0},{4,7},{5,6},{6,5},{7,4},{8,11},{9,10},{10,... | collective-permute-start | bytes 61448 | tf_op jit(solution)/shard_map/ppermute | solution.py:23
  26.3 3.8 %collective-permute-start.8 = (f32[40,128]{1,0:T(8,128)S(1)}, f32[40,128]{1,0:T(8,128)S(1)}, u32[]{:S(2)}, u32[]{:S(2)}) collective-permute-start(f32[40,128]{1,0:T(8,128)S(1)} %get-tuple-element.22), channel_id=1, source_target_pairs={{0,2},{1,3},{2,0},{3,1},{4,6},{5,7},{6,4},{7,5},{8,10},{9,11},{10,... | collective-permute-start | bytes 61448 | tf_op jit(solution)/shard_map/ppermute | solution.py:23
  26.3 3.8 %collective-permute-start.9 = (f32[40,128]{1,0:T(8,128)S(1)}, f32[40,128]{1,0:T(8,128)S(1)}, u32[]{:S(2)}, u32[]{:S(2)}) collective-permute-start(f32[40,128]{1,0:T(8,128)S(1)} %get-tuple-element.21), channel_id=1, source_target_pairs={{0,1},{1,0},{2,3},{3,2},{4,5},{5,4},{6,7},{7,6},{8,9},{9,8},{10,11... | collective-permute-start | bytes 61448 | tf_op jit(solution)/shard_map/ppermute | solution.py:23

commit v6 on v5

--- a/solution.py
+++ b/solution.py
@@ -189,8 +189,9 @@
     left = held[...]
     place = place_ref[...].astype(jnp.bfloat16)
     tiles = jnp.zeros((rows_dev * slots, BLK), jnp.float32)
+    most = float(jnp.finfo(jnp.bfloat16).max)
     for _ in range(3):
-        part = left.astype(jnp.bfloat16)
+        part = jnp.clip(left, -most, most).astype(jnp.bfloat16)
         tiles += jnp.dot(place, part, preferred_element_type=jnp.float32)
         left -= part.astype(jnp.float32)
     valid = jnp.sum(place_ref[...], axis=1, keepdims=True) > 0

time: 31 us -> 31 us (level)
  no operation moved by 1% of the time
where the time goes in v6:
time: 31 us; the launch traced here: 30.9 us
  starting transfers between devices  16.6 us (54%)
  Pallas kernels  6.97 us (22%)
  waiting for transfers between devices  6.03 us (19%)
  local copies, waits for them, and re-layouts  1.12 us (4%)
    ppermute x10, starting transfers between devices, exchange(): return lax.ppermute(x, 'vocab', [(i, i ^ mask) for i in range(n)])  16.6 us
    ppermute x10, waiting for transfers between devices, exchange(): return lax.ppermute(x, 'vocab', [(i, i ^ mask) for i in range(n)])  6.03 us
    pallas_call x1, Pallas kernels, body(): pl.pallas_call(functools.partial(score_kernel, n), out_shape=[jax.ShapeDt...  3.81 us
    pallas_call x1, Pallas kernels, body(): pl.pallas_call(functools.partial(index_kernel, n, rows_dev, blocks_dev),...  2.35 us
    unnamed x10, local copies, waits for them, and re-layouts  1.11 us
    pallas_call x1, Pallas kernels, body(): pl.pallas_call(functools.partial(place_kernel, n, rows_dev, slots), out_s...  0.81 us
  transfers between devices with their start and end apart: 10, of which 7 were waited for; matrix products, arithmetic and copies ran while one was open for 0% of the time, Pallas kernels for 8%

profile of v6, /device:TPU:0, one launch (start us, length us, event | category | flops | bytes accessed | tf_op | source)
XLA Modules:
  0.0 30.9 jit_solution(7933861987494887892)
XLA Ops:
  0.0 4.0 %collective-permute-start = (bf16[8,4096]{1,0:T(8,128)(2,1)}, bf16[8,4096]{1,0:T(8,128)(2,1)S(1)}, u32[]{:S(2)}, u32[]{:S(2)}) collective-permute-start(bf16[8,4096]{1,0:T(8,128)(2,1)} %param.5), channel_id=1, source_target_pairs={{0,4},{1,5},{2,6},{3,7},{4,0},{5,1},{6,2},{7,3},{8,12},{9,13},{10,... | collective-permute-start | bytes 196616 | tf_op jit(solution)/shard_map/ppermute | solution.py:23
  4.0 1.6 %collective-permute-start.1 = (bf16[8,4096]{1,0:T(8,128)(2,1)}, bf16[8,4096]{1,0:T(8,128)(2,1)S(1)}, u32[]{:S(2)}, u32[]{:S(2)}) collective-permute-start(bf16[8,4096]{1,0:T(8,128)(2,1)} %param.5), channel_id=1, source_target_pairs={{0,2},{1,3},{2,0},{3,1},{4,6},{5,7},{6,4},{7,5},{8,10},{9,11},{10,... | collective-permute-start | bytes 196616 | tf_op jit(solution)/shard_map/ppermute | solution.py:23
  5.6 1.5 %collective-permute-start.2 = (bf16[8,4096]{1,0:T(8,128)(2,1)}, bf16[8,4096]{1,0:T(8,128)(2,1)S(1)}, u32[]{:S(2)}, u32[]{:S(2)}) collective-permute-start(bf16[8,4096]{1,0:T(8,128)(2,1)} %param.5), channel_id=1, source_target_pairs={{0,1},{1,0},{2,3},{3,2},{4,5},{5,4},{6,7},{7,6},{8,9},{9,8},{10,11... | collective-permute-start | bytes 196616 | tf_op jit(solution)/shard_map/ppermute | solution.py:23
  7.1 0.0 copy-start.1
  7.1 0.0 copy-start
  7.2 0.1 collective-permute-done.after
  7.3 0.7 %copy-done.1 = bf16[8,4096]{1,0:T(8,128)(2,1)S(1)} copy-done((bf16[8,4096]{1,0:T(8,128)(2,1)S(1)}, bf16[8,4096]{1,0:T(8,128)(2,1)}, u32[]{:S(2)}) %copy-start.1) | copy-done | bytes 65560
  8.0 1.7 %collective-permute-start.3 = (bf16[16,4096]{1,0:T(8,128)(2,1)S(1)}, bf16[16,4096]{1,0:T(8,128)(2,1)S(1)}, u32[]{:S(2)}, u32[]{:S(2)}) collective-permute-start(bf16[16,4096]{1,0:T(8,128)(2,1)S(1)} %pad_maximum_fusion), channel_id=1, source_target_pairs={{0,3},{1,2},{2,1},{3,0},{4,7},{5,6},{6,5},{7,4},{8,11},{9,10},{10,... | collective-permute-start | bytes 393224 | tf_op jit(solution)/shard_map/ppermute | solution.py:23
  9.7 1.0 %collective-permute-start.4 = (bf16[8,4096]{1,0:T(8,128)(2,1)S(1)}, bf16[8,4096]{1,0:T(8,128)(2,1)S(1)}, u32[]{:S(2)}, u32[]{:S(2)}) collective-permute-start(bf16[8,4096]{1,0:T(8,128)(2,1)S(1)} %collective-permute-done.after), channel_id=1, source_target_pairs={{0,2},{1,3},{2,0},{3,1},{4,6},{5,7},{6,4},{7,5},{8,10},{9,11},{10,... | collective-permute-start | bytes 196616 | tf_op jit(solution)/shard_map/ppermute | solution.py:23
  10.7 0.9 %collective-permute-start.5 = (bf16[8,4096]{1,0:T(8,128)(2,1)S(1)}, bf16[8,4096]{1,0:T(8,128)(2,1)S(1)}, u32[]{:S(2)}, u32[]{:S(2)}) collective-permute-start(bf16[8,4096]{1,0:T(8,128)(2,1)S(1)} %collective-permute-done.after), channel_id=1, source_target_pairs={{0,1},{1,0},{2,3},{3,2},{4,5},{5,4},{6,7},{7,6},{8,9},{9,8},{10,11... | collective-permute-start | bytes 196616 | tf_op jit(solution)/shard_map/ppermute | solution.py:23
  11.6 0.0 collective-permute-done.1
  11.6 0.0 collective-permute-done.2
  11.6 2.3 %index.1 = (s32[16,8]{1,0:T(8,128)S(1)}, s32[1,128]{1,0:T(1,128)S(1)}, f32[128,128]{1,0:T(8,128)S(1)}) custom-call(s32[1]{0:T(128)} %bitcast.me_ref, s32[16,64]{1,0:T(8,128)} %bitcast.4, s32[1,64]{1,0:T(1,128)} %bitcast.5, s32[1,64]{1,0:T(1,128)} %bitcast.6, s32[8,128]{1,0:T(8,128)S(1)} %mark.1, bf16[8,4096]{1,0:T(8,128)(2,1)S(1)} %collective-permute-done.after), custom_call_target="tpu_custom_call" | custom-call | tf_op jit(solution)/shard_map/index/pallas_call | solution.py:237
  14.0 0.1 collective-permute-done.3
  14.1 0.3 collective-permute-done.4
  14.4 0.6 %collective-permute-done.5 = bf16[8,4096]{1,0:T(8,128)(2,1)S(1)} collective-permute-done((bf16[8,4096]{1,0:T(8,128)(2,1)S(1)}, bf16[8,4096]{1,0:T(8,128)(2,1)S(1)}, u32[]{:S(2)}, u32[]{:S(2)}) %collective-permute-start.5) | collective-permute-done | bytes 65568 | tf_op jit(solution)/shard_map/ppermute | solution.py:23
  15.0 0.4 %copy-done = bf16[4096,3072]{1,0:T(8,128)(2,1)S(1)} copy-done((bf16[4096,3072]{1,0:T(8,128)(2,1)S(1)}, bf16[4096,3072]{1,0:T(8,128)(2,1)}, u32[]{:S(2)}) %copy-start) | copy-done | bytes 25165848
  15.4 3.8 %score.1 = (f32[72,128]{1,0:T(8,128)S(1)}, f32[72,128]{1,0:T(8,128)S(1)}) custom-call(s32[1]{0:T(128)} %bitcast.me_ref, s32[16,8]{1,0:T(8,128)S(1)} %get-tuple-element.11.src_vmem, s32[1,128]{1,0:T(1,128)S(1)} %get-tuple-element.12.rows_ref, bf16[64,4096]{1,0:T(8,128)(2,1)S(1)} %constant_dynamic-update-slice_fusion.x_ref, bf16[4096,3072]{1,0:T(8,128)(2,1)S(1)} %copy-done), custom_call_target="tpu_custom_call" | custom-call | tf_op jit(solution)/shard_map/score/pallas_call | solution.py:268
  19.2 2.3 %collective-permute-start.6 = (f32[72,128]{1,0:T(8,128)S(1)}, f32[72,128]{1,0:T(8,128)S(1)}, u32[]{:S(2)}, u32[]{:S(2)}) collective-permute-start(f32[72,128]{1,0:T(8,128)S(1)} %get-tuple-element.14), channel_id=1, source_target_pairs={{0,4},{1,5},{2,6},{3,7},{4,0},{5,1},{6,2},{7,3},{8,12},{9,13},{10,... | collective-permute-start | bytes 110600 | tf_op jit(solution)/shard_map/ppermute | solution.py:23
  21.5 2.6 %collective-permute-done.6.refs_1_ = f32[72,128]{1,0:T(8,128)S(1)} collective-permute-done((f32[72,128]{1,0:T(8,128)S(1)}, f32[72,128]{1,0:T(8,128)S(1)}, u32[]{:S(2)}, u32[]{:S(2)}) %collective-permute-start.6) | collective-permute-done | bytes 36896 | tf_op jit(solution)/shard_map/ppermute | solution.py:23
  24.1 0.1 slice_select_fusion
  24.2 2.0 %collective-permute-start.7 = (f32[40,128]{1,0:T(8,128)S(1)}, f32[40,128]{1,0:T(8,128)S(1)}, u32[]{:S(2)}, u32[]{:S(2)}) collective-permute-start(f32[40,128]{1,0:T(8,128)S(1)} %get-tuple-element.23), channel_id=1, source_target_pairs={{0,3},{1,2},{2,1},{3,0},{4,7},{5,6},{6,5},{7,4},{8,11},{9,10},{10,... | collective-permute-start | bytes 61448 | tf_op jit(solution)/shard_map/ppermute | solution.py:23
  26.3 0.0 collective-permute-start.8
  26.3 1.5 %collective-permute-start.9 = (f32[40,128]{1,0:T(8,128)S(1)}, f32[40,128]{1,0:T(8,128)S(1)}, u32[]{:S(2)}, u32[]{:S(2)}) collective-permute-start(f32[40,128]{1,0:T(8,128)S(1)} %get-tuple-element.21), channel_id=1, source_target_pairs={{0,1},{1,0},{2,3},{3,2},{4,5},{5,4},{6,7},{7,6},{8,9},{9,8},{10,11... | collective-permute-start | bytes 61448 | tf_op jit(solution)/shard_map/ppermute | solution.py:23
  27.8 1.2 %collective-permute-done.7.refs_2_ = f32[40,128]{1,0:T(8,128)S(1)} collective-permute-done((f32[40,128]{1,0:T(8,128)S(1)}, f32[40,128]{1,0:T(8,128)S(1)}, u32[]{:S(2)}, u32[]{:S(2)}) %collective-permute-start.7) | collective-permute-done | bytes 20512 | tf_op jit(solution)/shard_map/ppermute | solution.py:23
  29.0 1.1 %collective-permute-done.8.refs_3_ = f32[40,128]{1,0:T(8,128)S(1)} collective-permute-done((f32[40,128]{1,0:T(8,128)S(1)}, f32[40,128]{1,0:T(8,128)S(1)}, u32[]{:S(2)}, u32[]{:S(2)}) %collective-permute-start.8) | collective-permute-done | bytes 20512 | tf_op jit(solution)/shard_map/ppermute | solution.py:23
  30.0 0.0 collective-permute-done.9.refs_4_
  30.1 0.8 %place.1 = f32[8,16,128]{2,1,0:T(8,128)} custom-call(s32[1]{0:T(128)} %bitcast.me_ref, f32[128,128]{1,0:T(8,128)S(1)} %get-tuple-element.10.place_ref, f32[72,128]{1,0:T(8,128)S(1)} %get-tuple-element.13.refs_0_, f32[72,128]{1,0:T(8,128)S(1)} %collective-permute-done.6.refs_1_, f32[40,128]{1,0:T(8,128)S(1)} %collective-permute-done.7.refs_2_, ...), custom_call_target="tpu_custom_call" | custom-call | tf_op jit(solution)/shard_map/place/pallas_call | solution.py:292
  (14 shorter events, 0.1 us)
Async XLA Ops:
  0.0 7.3 %collective-permute-start = (bf16[8,4096]{1,0:T(8,128)(2,1)}, bf16[8,4096]{1,0:T(8,128)(2,1)S(1)}, u32[]{:S(2)}, u32[]{:S(2)}) collective-permute-start(bf16[8,4096]{1,0:T(8,128)(2,1)} %param.5), channel_id=1, source_target_pairs={{0,4},{1,5},{2,6},{3,7},{4,0},{5,1},{6,2},{7,3},{8,12},{9,13},{10,... | collective-permute-start | bytes 196616 | tf_op jit(solution)/shard_map/ppermute | solution.py:23
  4.0 7.5 %collective-permute-start.1 = (bf16[8,4096]{1,0:T(8,128)(2,1)}, bf16[8,4096]{1,0:T(8,128)(2,1)S(1)}, u32[]{:S(2)}, u32[]{:S(2)}) collective-permute-start(bf16[8,4096]{1,0:T(8,128)(2,1)} %param.5), channel_id=1, source_target_pairs={{0,2},{1,3},{2,0},{3,1},{4,6},{5,7},{6,4},{7,5},{8,10},{9,11},{10,... | collective-permute-start | bytes 196616 | tf_op jit(solution)/shard_map/ppermute | solution.py:23
  5.6 6.0 %collective-permute-start.2 = (bf16[8,4096]{1,0:T(8,128)(2,1)}, bf16[8,4096]{1,0:T(8,128)(2,1)S(1)}, u32[]{:S(2)}, u32[]{:S(2)}) collective-permute-start(bf16[8,4096]{1,0:T(8,128)(2,1)} %param.5), channel_id=1, source_target_pairs={{0,1},{1,0},{2,3},{3,2},{4,5},{5,4},{6,7},{7,6},{8,9},{9,8},{10,11... | collective-permute-start | bytes 196616 | tf_op jit(solution)/shard_map/ppermute | solution.py:23
  7.1 0.9 %copy-start.1 = (bf16[8,4096]{1,0:T(8,128)(2,1)S(1)}, bf16[8,4096]{1,0:T(8,128)(2,1)}, u32[]{:S(2)}) copy-start(bf16[8,4096]{1,0:T(8,128)(2,1)} %param.5) | copy-start | bytes 196612
  7.1 8.2 %copy-start = (bf16[4096,3072]{1,0:T(8,128)(2,1)S(1)}, bf16[4096,3072]{1,0:T(8,128)(2,1)}, u32[]{:S(2)}) copy-start(bf16[4096,3072]{1,0:T(8,128)(2,1)} %head_ref.1) | copy-start | bytes 75497472
  8.0 6.1 %collective-permute-start.3 = (bf16[16,4096]{1,0:T(8,128)(2,1)S(1)}, bf16[16,4096]{1,0:T(8,128)(2,1)S(1)}, u32[]{:S(2)}, u32[]{:S(2)}) collective-permute-start(bf16[16,4096]{1,0:T(8,128)(2,1)S(1)} %pad_maximum_fusion), channel_id=1, source_target_pairs={{0,3},{1,2},{2,1},{3,0},{4,7},{5,6},{6,5},{7,4},{8,11},{9,10},{10,... | collective-permute-start | bytes 393224 | tf_op jit(solution)/shard_map/ppermute | solution.py:23
  9.7 4.7 %collective-permute-start.4 = (bf16[8,4096]{1,0:T(8,128)(2,1)S(1)}, bf16[8,4096]{1,0:T(8,128)(2,1)S(1)}, u32[]{:S(2)}, u32[]{:S(2)}) collective-permute-start(bf16[8,4096]{1,0:T(8,128)(2,1)S(1)} %collective-permute-done.after), channel_id=1, source_target_pairs={{0,2},{1,3},{2,0},{3,1},{4,6},{5,7},{6,4},{7,5},{8,10},{9,11},{10,... | collective-permute-start | bytes 196616 | tf_op jit(solution)/shard_map/ppermute | solution.py:23
  10.7 4.3 %collective-permute-start.5 = (bf16[8,4096]{1,0:T(8,128)(2,1)S(1)}, bf16[8,4096]{1,0:T(8,128)(2,1)S(1)}, u32[]{:S(2)}, u32[]{:S(2)}) collective-permute-start(bf16[8,4096]{1,0:T(8,128)(2,1)S(1)} %collective-permute-done.after), channel_id=1, source_target_pairs={{0,1},{1,0},{2,3},{3,2},{4,5},{5,4},{6,7},{7,6},{8,9},{9,8},{10,11... | collective-permute-start | bytes 196616 | tf_op jit(solution)/shard_map/ppermute | solution.py:23
  19.2 4.9 %collective-permute-start.6 = (f32[72,128]{1,0:T(8,128)S(1)}, f32[72,128]{1,0:T(8,128)S(1)}, u32[]{:S(2)}, u32[]{:S(2)}) collective-permute-start(f32[72,128]{1,0:T(8,128)S(1)} %get-tuple-element.14), channel_id=1, source_target_pairs={{0,4},{1,5},{2,6},{3,7},{4,0},{5,1},{6,2},{7,3},{8,12},{9,13},{10,... | collective-permute-start | bytes 110600 | tf_op jit(solution)/shard_map/ppermute | solution.py:23
  24.2 4.7 %collective-permute-start.7 = (f32[40,128]{1,0:T(8,128)S(1)}, f32[40,128]{1,0:T(8,128)S(1)}, u32[]{:S(2)}, u32[]{:S(2)}) collective-permute-start(f32[40,128]{1,0:T(8,128)S(1)} %get-tuple-element.23), channel_id=1, source_target_pairs={{0,3},{1,2},{2,1},{3,0},{4,7},{5,6},{6,5},{7,4},{8,11},{9,10},{10,... | collective-permute-start | bytes 61448 | tf_op jit(solution)/shard_map/ppermute | solution.py:23
  26.3 3.8 %collective-permute-start.8 = (f32[40,128]{1,0:T(8,128)S(1)}, f32[40,128]{1,0:T(8,128)S(1)}, u32[]{:S(2)}, u32[]{:S(2)}) collective-permute-start(f32[40,128]{1,0:T(8,128)S(1)} %get-tuple-element.22), channel_id=1, source_target_pairs={{0,2},{1,3},{2,0},{3,1},{4,6},{5,7},{6,4},{7,5},{8,10},{9,11},{10,... | collective-permute-start | bytes 61448 | tf_op jit(solution)/shard_map/ppermute | solution.py:23
  26.3 3.8 %collective-permute-start.9 = (f32[40,128]{1,0:T(8,128)S(1)}, f32[40,128]{1,0:T(8,128)S(1)}, u32[]{:S(2)}, u32[]{:S(2)}) collective-permute-start(f32[40,128]{1,0:T(8,128)S(1)} %get-tuple-element.21), channel_id=1, source_target_pairs={{0,1},{1,0},{2,3},{3,2},{4,5},{5,4},{6,7},{7,6},{8,9},{9,8},{10,11... | collective-permute-start | bytes 61448 | tf_op jit(solution)/shard_map/ppermute | solution.py:23

commit v7 on v6

--- a/solution.py
+++ b/solution.py
@@ -12,8 +12,8 @@
 NEAR = 4
 EARLY = (2, 1)
 LATE = (3, 2, 1)
-FIRST = (0, 4)
-SECOND = (0, 3, 2, 1)
+FIRST = (0, 3, 2, 1)
+SECOND = (0, 4)
 GROUP = 2
 ROWS = 128
 PAD = 8

time: 31 us -> 30.9 us (level)
  waiting for transfers between devices: 6.03 us -> 5.35 us
  starting transfers between devices: 16.6 us -> 17.2 us
    ppermute x10, waiting for transfers between devices: 6.03 us -> 5.35 us  [exchange(): return lax.ppermute(x, 'vocab', [(i, i ^ mask) for i in range(n)])]
    ppermute x10, starting transfers between devices: 16.6 us -> 17.2 us  [exchange(): return lax.ppermute(x, 'vocab', [(i, i ^ mask) for i in range(n)])]
    unnamed x10 -> x14, local copies, waits for them, and re-layouts: 1.11 us -> 1.12 us
  transfers between devices with their start and end apart: 10 -> 10, of which waited for: 7 -> 8; matrix products, arithmetic and copies ran while one was open for 0% -> 0% of each run, Pallas kernels for 8% -> 8%
where the time goes in v7:
time: 30.9 us; the launch traced here: 30.8 us
  starting transfers between devices  17.2 us (56%)
  Pallas kernels  6.96 us (23%)
  waiting for transfers between devices  5.35 us (17%)
  local copies, waits for them, and re-layouts  1.12 us (4%)
    ppermute x10, starting transfers between devices, exchange(): return lax.ppermute(x, 'vocab', [(i, i ^ mask) for i in range(n)])  17.2 us
    ppermute x10, waiting for transfers between devices, exchange(): return lax.ppermute(x, 'vocab', [(i, i ^ mask) for i in range(n)])  5.35 us
    pallas_call x1, Pallas kernels, body(): pl.pallas_call(functools.partial(score_kernel, n), out_shape=[jax.ShapeDt...  3.8 us
    pallas_call x1, Pallas kernels, body(): pl.pallas_call(functools.partial(index_kernel, n, rows_dev, blocks_dev),...  2.35 us
    unnamed x14, local copies, waits for them, and re-layouts  1.12 us
    pallas_call x1, Pallas kernels, body(): pl.pallas_call(functools.partial(place_kernel, n, rows_dev, slots), out_s...  0.81 us
  transfers between devices with their start and end apart: 10, of which 8 were waited for; matrix products, arithmetic and copies ran while one was open for 0% of the time, Pallas kernels for 8%

profile of v7, /device:TPU:0, one launch (start us, length us, event | category | flops | bytes accessed | tf_op | source)
XLA Modules:
  0.0 30.8 jit_solution(9182742827364760317)
XLA Ops:
  0.0 4.0 %collective-permute-start = (bf16[8,4096]{1,0:T(8,128)(2,1)}, bf16[8,4096]{1,0:T(8,128)(2,1)S(1)}, u32[]{:S(2)}, u32[]{:S(2)}) collective-permute-start(bf16[8,4096]{1,0:T(8,128)(2,1)} %param.5), channel_id=1, source_target_pairs={{0,4},{1,5},{2,6},{3,7},{4,0},{5,1},{6,2},{7,3},{8,12},{9,13},{10,... | collective-permute-start | bytes 196616 | tf_op jit(solution)/shard_map/ppermute | solution.py:23
  4.0 1.6 %collective-permute-start.1 = (bf16[8,4096]{1,0:T(8,128)(2,1)}, bf16[8,4096]{1,0:T(8,128)(2,1)S(1)}, u32[]{:S(2)}, u32[]{:S(2)}) collective-permute-start(bf16[8,4096]{1,0:T(8,128)(2,1)} %param.5), channel_id=1, source_target_pairs={{0,2},{1,3},{2,0},{3,1},{4,6},{5,7},{6,4},{7,5},{8,10},{9,11},{10,... | collective-permute-start | bytes 196616 | tf_op jit(solution)/shard_map/ppermute | solution.py:23
  5.6 1.5 %collective-permute-start.2 = (bf16[8,4096]{1,0:T(8,128)(2,1)}, bf16[8,4096]{1,0:T(8,128)(2,1)S(1)}, u32[]{:S(2)}, u32[]{:S(2)}) collective-permute-start(bf16[8,4096]{1,0:T(8,128)(2,1)} %param.5), channel_id=1, source_target_pairs={{0,1},{1,0},{2,3},{3,2},{4,5},{5,4},{6,7},{7,6},{8,9},{9,8},{10,11... | collective-permute-start | bytes 196616 | tf_op jit(solution)/shard_map/ppermute | solution.py:23
  7.1 0.0 copy-start.1
  7.1 0.0 copy-start
  7.2 0.1 collective-permute-done.after
  7.3 0.7 %copy-done.1 = bf16[8,4096]{1,0:T(8,128)(2,1)S(1)} copy-done((bf16[8,4096]{1,0:T(8,128)(2,1)S(1)}, bf16[8,4096]{1,0:T(8,128)(2,1)}, u32[]{:S(2)}) %copy-start.1) | copy-done | bytes 65560
  8.0 1.7 %collective-permute-start.3 = (bf16[16,4096]{1,0:T(8,128)(2,1)S(1)}, bf16[16,4096]{1,0:T(8,128)(2,1)S(1)}, u32[]{:S(2)}, u32[]{:S(2)}) collective-permute-start(bf16[16,4096]{1,0:T(8,128)(2,1)S(1)} %pad_maximum_fusion), channel_id=1, source_target_pairs={{0,3},{1,2},{2,1},{3,0},{4,7},{5,6},{6,5},{7,4},{8,11},{9,10},{10,... | collective-permute-start | bytes 393224 | tf_op jit(solution)/shard_map/ppermute | solution.py:23
  9.7 1.0 %collective-permute-start.4 = (bf16[8,4096]{1,0:T(8,128)(2,1)S(1)}, bf16[8,4096]{1,0:T(8,128)(2,1)S(1)}, u32[]{:S(2)}, u32[]{:S(2)}) collective-permute-start(bf16[8,4096]{1,0:T(8,128)(2,1)S(1)} %collective-permute-done.after), channel_id=1, source_target_pairs={{0,2},{1,3},{2,0},{3,1},{4,6},{5,7},{6,4},{7,5},{8,10},{9,11},{10,... | collective-permute-start | bytes 196616 | tf_op jit(solution)/shard_map/ppermute | solution.py:23
  10.7 0.9 %collective-permute-start.5 = (bf16[8,4096]{1,0:T(8,128)(2,1)S(1)}, bf16[8,4096]{1,0:T(8,128)(2,1)S(1)}, u32[]{:S(2)}, u32[]{:S(2)}) collective-permute-start(bf16[8,4096]{1,0:T(8,128)(2,1)S(1)} %collective-permute-done.after), channel_id=1, source_target_pairs={{0,1},{1,0},{2,3},{3,2},{4,5},{5,4},{6,7},{7,6},{8,9},{9,8},{10,11... | collective-permute-start | bytes 196616 | tf_op jit(solution)/shard_map/ppermute | solution.py:23
  11.6 0.0 collective-permute-done.1
  11.6 0.0 collective-permute-done.2
  11.6 2.3 %index.1 = (s32[16,8]{1,0:T(8,128)S(1)}, s32[1,128]{1,0:T(1,128)S(1)}, f32[128,128]{1,0:T(8,128)S(1)}) custom-call(s32[1]{0:T(128)} %bitcast.me_ref, s32[16,64]{1,0:T(8,128)} %bitcast.4, s32[1,64]{1,0:T(1,128)} %bitcast.5, s32[1,64]{1,0:T(1,128)} %bitcast.6, s32[8,128]{1,0:T(8,128)S(1)} %mark.1, bf16[8,4096]{1,0:T(8,128)(2,1)S(1)} %collective-permute-done.after), custom_call_target="tpu_custom_call" | custom-call | tf_op jit(solution)/shard_map/index/pallas_call | solution.py:237
  14.0 0.1 collective-permute-done.3
  14.1 0.3 collective-permute-done.4
  14.4 0.6 %collective-permute-done.5 = bf16[8,4096]{1,0:T(8,128)(2,1)S(1)} collective-permute-done((bf16[8,4096]{1,0:T(8,128)(2,1)S(1)}, bf16[8,4096]{1,0:T(8,128)(2,1)S(1)}, u32[]{:S(2)}, u32[]{:S(2)}) %collective-permute-start.5) | collective-permute-done | bytes 65568 | tf_op jit(solution)/shard_map/ppermute | solution.py:23
  15.0 0.4 %copy-done = bf16[4096,3072]{1,0:T(8,128)(2,1)S(1)} copy-done((bf16[4096,3072]{1,0:T(8,128)(2,1)S(1)}, bf16[4096,3072]{1,0:T(8,128)(2,1)}, u32[]{:S(2)}) %copy-start) | copy-done | bytes 25165848
  15.4 3.8 %score.1 = (f32[40,128]{1,0:T(8,128)S(1)}, f32[40,128]{1,0:T(8,128)S(1)}, f32[40,128]{1,0:T(8,128)S(1)}, f32[40,128]{1,0:T(8,128)S(1)}) custom-call(s32[1]{0:T(128)} %bitcast.me_ref, s32[16,8]{1,0:T(8,128)S(1)} %get-tuple-element.13.src_vmem, s32[1,128]{1,0:T(1,128)S(1)} %get-tuple-element.14.rows_ref, ...), custom_call_target="tpu_custom_call" | custom-call | tf_op jit(solution)/shard_map/score/pallas_call | solution.py:268
  19.2 1.2 %collective-permute-start.6 = (f32[40,128]{1,0:T(8,128)S(1)}, f32[40,128]{1,0:T(8,128)S(1)}, u32[]{:S(2)}, u32[]{:S(2)}) collective-permute-start(f32[40,128]{1,0:T(8,128)S(1)} %get-tuple-element.16), channel_id=1, source_target_pairs={{0,3},{1,2},{2,1},{3,0},{4,7},{5,6},{6,5},{7,4},{8,11},{9,10},{10,... | collective-permute-start | bytes 61448 | tf_op jit(solution)/shard_map/ppermute | solution.py:23
  20.4 0.9 %collective-permute-start.7 = (f32[40,128]{1,0:T(8,128)S(1)}, f32[40,128]{1,0:T(8,128)S(1)}, u32[]{:S(2)}, u32[]{:S(2)}) collective-permute-start(f32[40,128]{1,0:T(8,128)S(1)} %get-tuple-element.17), channel_id=1, source_target_pairs={{0,2},{1,3},{2,0},{3,1},{4,6},{5,7},{6,4},{7,5},{8,10},{9,11},{10,... | collective-permute-start | bytes 61448 | tf_op jit(solution)/shard_map/ppermute | solution.py:23
  21.2 1.5 %collective-permute-start.8 = (f32[40,128]{1,0:T(8,128)S(1)}, f32[40,128]{1,0:T(8,128)S(1)}, u32[]{:S(2)}, u32[]{:S(2)}) collective-permute-start(f32[40,128]{1,0:T(8,128)S(1)} %get-tuple-element.18), channel_id=1, source_target_pairs={{0,1},{1,0},{2,3},{3,2},{4,5},{5,4},{6,7},{7,6},{8,9},{9,8},{10,11... | collective-permute-start | bytes 61448 | tf_op jit(solution)/shard_map/ppermute | solution.py:23
  22.8 1.2 %collective-permute-done.6.refs_1_ = f32[40,128]{1,0:T(8,128)S(1)} collective-permute-done((f32[40,128]{1,0:T(8,128)S(1)}, f32[40,128]{1,0:T(8,128)S(1)}, u32[]{:S(2)}, u32[]{:S(2)}) %collective-permute-start.6) | collective-permute-done | bytes 20512 | tf_op jit(solution)/shard_map/ppermute | solution.py:23
  23.9 0.2 collective-permute-done.7.refs_2_
  24.2 0.8 %collective-permute-done.8.refs_3_ = f32[40,128]{1,0:T(8,128)S(1)} collective-permute-done((f32[40,128]{1,0:T(8,128)S(1)}, f32[40,128]{1,0:T(8,128)S(1)}, u32[]{:S(2)}, u32[]{:S(2)}) %collective-permute-start.8) | collective-permute-done | bytes 20512 | tf_op jit(solution)/shard_map/ppermute | solution.py:23
  25.0 0.1 constant_dynamic-update-slice_fusion.7
  25.1 2.9 %collective-permute-start.9 = (f32[72,128]{1,0:T(8,128)S(1)}, f32[72,128]{1,0:T(8,128)S(1)}, u32[]{:S(2)}, u32[]{:S(2)}) collective-permute-start(f32[72,128]{1,0:T(8,128)S(1)} %constant_dynamic-update-slice_fusion.7), channel_id=1, source_target_pairs={{0,4},{1,5},{2,6},{3,7},{4,0},{5,1},{6,2},{7,3},{8,12},{9,13},{10,... | collective-permute-start | bytes 110600 | tf_op jit(solution)/shard_map/ppermute | solution.py:23
  28.0 1.9 %collective-permute-done.9.refs_4_ = f32[72,128]{1,0:T(8,128)S(1)} collective-permute-done((f32[72,128]{1,0:T(8,128)S(1)}, f32[72,128]{1,0:T(8,128)S(1)}, u32[]{:S(2)}, u32[]{:S(2)}) %collective-permute-start.9) | collective-permute-done | bytes 36896 | tf_op jit(solution)/shard_map/ppermute | solution.py:23
  30.0 0.8 %place.1 = f32[8,16,128]{2,1,0:T(8,128)} custom-call(s32[1]{0:T(128)} %bitcast.me_ref, f32[128,128]{1,0:T(8,128)S(1)} %get-tuple-element.12.place_ref, f32[40,128]{1,0:T(8,128)S(1)} %get-tuple-element.15.refs_0_, f32[40,128]{1,0:T(8,128)S(1)} %collective-permute-done.6.refs_1_, f32[40,128]{1,0:T(8,128)S(1)} %collective-permute-done.7.refs_2_, ...), custom_call_target="tpu_custom_call" | custom-call | tf_op jit(solution)/shard_map/place/pallas_call | solution.py:292
  (15 shorter events, 0.1 us)
Async XLA Ops:
  0.0 7.3 %collective-permute-start = (bf16[8,4096]{1,0:T(8,128)(2,1)}, bf16[8,4096]{1,0:T(8,128)(2,1)S(1)}, u32[]{:S(2)}, u32[]{:S(2)}) collective-permute-start(bf16[8,4096]{1,0:T(8,128)(2,1)} %param.5), channel_id=1, source_target_pairs={{0,4},{1,5},{2,6},{3,7},{4,0},{5,1},{6,2},{7,3},{8,12},{9,13},{10,... | collective-permute-start | bytes 196616 | tf_op jit(solution)/shard_map/ppermute | solution.py:23
  4.0 7.5 %collective-permute-start.1 = (bf16[8,4096]{1,0:T(8,128)(2,1)}, bf16[8,4096]{1,0:T(8,128)(2,1)S(1)}, u32[]{:S(2)}, u32[]{:S(2)}) collective-permute-start(bf16[8,4096]{1,0:T(8,128)(2,1)} %param.5), channel_id=1, source_target_pairs={{0,2},{1,3},{2,0},{3,1},{4,6},{5,7},{6,4},{7,5},{8,10},{9,11},{10,... | collective-permute-start | bytes 196616 | tf_op jit(solution)/shard_map/ppermute | solution.py:23
  5.6 6.0 %collective-permute-start.2 = (bf16[8,4096]{1,0:T(8,128)(2,1)}, bf16[8,4096]{1,0:T(8,128)(2,1)S(1)}, u32[]{:S(2)}, u32[]{:S(2)}) collective-permute-start(bf16[8,4096]{1,0:T(8,128)(2,1)} %param.5), channel_id=1, source_target_pairs={{0,1},{1,0},{2,3},{3,2},{4,5},{5,4},{6,7},{7,6},{8,9},{9,8},{10,11... | collective-permute-start | bytes 196616 | tf_op jit(solution)/shard_map/ppermute | solution.py:23
  7.1 0.9 %copy-start.1 = (bf16[8,4096]{1,0:T(8,128)(2,1)S(1)}, bf16[8,4096]{1,0:T(8,128)(2,1)}, u32[]{:S(2)}) copy-start(bf16[8,4096]{1,0:T(8,128)(2,1)} %param.5) | copy-start | bytes 196612
  7.1 8.2 %copy-start = (bf16[4096,3072]{1,0:T(8,128)(2,1)S(1)}, bf16[4096,3072]{1,0:T(8,128)(2,1)}, u32[]{:S(2)}) copy-start(bf16[4096,3072]{1,0:T(8,128)(2,1)} %head_ref.1) | copy-start | bytes 75497472
  8.0 6.1 %collective-permute-start.3 = (bf16[16,4096]{1,0:T(8,128)(2,1)S(1)}, bf16[16,4096]{1,0:T(8,128)(2,1)S(1)}, u32[]{:S(2)}, u32[]{:S(2)}) collective-permute-start(bf16[16,4096]{1,0:T(8,128)(2,1)S(1)} %pad_maximum_fusion), channel_id=1, source_target_pairs={{0,3},{1,2},{2,1},{3,0},{4,7},{5,6},{6,5},{7,4},{8,11},{9,10},{10,... | collective-permute-start | bytes 393224 | tf_op jit(solution)/shard_map/ppermute | solution.py:23
  9.7 4.7 %collective-permute-start.4 = (bf16[8,4096]{1,0:T(8,128)(2,1)S(1)}, bf16[8,4096]{1,0:T(8,128)(2,1)S(1)}, u32[]{:S(2)}, u32[]{:S(2)}) collective-permute-start(bf16[8,4096]{1,0:T(8,128)(2,1)S(1)} %collective-permute-done.after), channel_id=1, source_target_pairs={{0,2},{1,3},{2,0},{3,1},{4,6},{5,7},{6,4},{7,5},{8,10},{9,11},{10,... | collective-permute-start | bytes 196616 | tf_op jit(solution)/shard_map/ppermute | solution.py:23
  10.7 4.3 %collective-permute-start.5 = (bf16[8,4096]{1,0:T(8,128)(2,1)S(1)}, bf16[8,4096]{1,0:T(8,128)(2,1)S(1)}, u32[]{:S(2)}, u32[]{:S(2)}) collective-permute-start(bf16[8,4096]{1,0:T(8,128)(2,1)S(1)} %collective-permute-done.after), channel_id=1, source_target_pairs={{0,1},{1,0},{2,3},{3,2},{4,5},{5,4},{6,7},{7,6},{8,9},{9,8},{10,11... | collective-permute-start | bytes 196616 | tf_op jit(solution)/shard_map/ppermute | solution.py:23
  19.2 4.7 %collective-permute-start.6 = (f32[40,128]{1,0:T(8,128)S(1)}, f32[40,128]{1,0:T(8,128)S(1)}, u32[]{:S(2)}, u32[]{:S(2)}) collective-permute-start(f32[40,128]{1,0:T(8,128)S(1)} %get-tuple-element.16), channel_id=1, source_target_pairs={{0,3},{1,2},{2,1},{3,0},{4,7},{5,6},{6,5},{7,4},{8,11},{9,10},{10,... | collective-permute-start | bytes 61448 | tf_op jit(solution)/shard_map/ppermute | solution.py:23
  20.4 3.8 %collective-permute-start.7 = (f32[40,128]{1,0:T(8,128)S(1)}, f32[40,128]{1,0:T(8,128)S(1)}, u32[]{:S(2)}, u32[]{:S(2)}) collective-permute-start(f32[40,128]{1,0:T(8,128)S(1)} %get-tuple-element.17), channel_id=1, source_target_pairs={{0,2},{1,3},{2,0},{3,1},{4,6},{5,7},{6,4},{7,5},{8,10},{9,11},{10,... | collective-permute-start | bytes 61448 | tf_op jit(solution)/shard_map/ppermute | solution.py:23
  21.2 3.8 %collective-permute-start.8 = (f32[40,128]{1,0:T(8,128)S(1)}, f32[40,128]{1,0:T(8,128)S(1)}, u32[]{:S(2)}, u32[]{:S(2)}) collective-permute-start(f32[40,128]{1,0:T(8,128)S(1)} %get-tuple-element.18), channel_id=1, source_target_pairs={{0,1},{1,0},{2,3},{3,2},{4,5},{5,4},{6,7},{7,6},{8,9},{9,8},{10,11... | collective-permute-start | bytes 61448 | tf_op jit(solution)/shard_map/ppermute | solution.py:23
  25.1 4.9 %collective-permute-start.9 = (f32[72,128]{1,0:T(8,128)S(1)}, f32[72,128]{1,0:T(8,128)S(1)}, u32[]{:S(2)}, u32[]{:S(2)}) collective-permute-start(f32[72,128]{1,0:T(8,128)S(1)} %constant_dynamic-update-slice_fusion.7), channel_id=1, source_target_pairs={{0,4},{1,5},{2,6},{3,7},{4,0},{5,1},{6,2},{7,3},{8,12},{9,13},{10,... | collective-permute-start | bytes 110600 | tf_op jit(solution)/shard_map/ppermute | solution.py:23
